TPU v7x, 32 devices: a whole 2x2x4 slice. The times are simulated.
32 devices in a mesh: expert: 8 (over z, y), segment: 4 (over x, core).
Axes of the slice: x: 2, y: 2, z: 4, core: 2. Of those that a mesh axis runs over, the one named last changes fastest.
Arguments:
- tokens: bfloat16 [4, 8, 128, 1664], P('segment', 'expert'), may hold values from -6 to 6
- route_ids: int32 [4, 8, 128, 2], P('segment', 'expert'), may hold values from 0 to 7, all different within a row; in each aligned block of 128 rows (0 to 127, 128 to 255, ..., all dimensions but the last counted through in order) at most 48 rows name the same one
- cotangent: bfloat16 [4, 8, 128, 1664], P('segment', 'expert'), may hold values from -6 to 6
- first_gain: float32 [1664], replicated, may hold values from 0.25 to 1.75
- in_projection: bfloat16 [1664, 2496], replicated, may hold values from -0.3125 to 0.3125
- out_projection: bfloat16 [832, 1664], replicated, may hold values from -0.21875 to 0.21875
- second_gain: float32 [1664], replicated, may hold values from 0.25 to 1.75
- router_weight: bfloat16 [1664, 8], replicated, may hold values from -0.15625 to 0.15625
- up_weight: bfloat16 [4, 8, 1664, 1024], P('segment', 'expert'), may hold values from -0.15625 to 0.15625
- down_weight: bfloat16 [4, 8, 1024, 1664], P('segment', 'expert'), may hold values from -0.09375 to 0.09375
Outputs:
- layer_out: bfloat16 [4, 8, 128, 1664], P('segment', 'expert')
- input_grad: bfloat16 [4, 8, 128, 1664], P('segment', 'expert')
Inputs may be any that keep to these rules, and one draw needn't show every extreme that they name: `route_ids`: the 2 experts of a token differ; among the 128 tokens of one image no expert is named more than 48 times, and in every draw some image names some expert exactly 48 times.
All inputs are finite; a program needn't handle non-finite values.
Results may differ from a plain program's by a relative error of at most 0.023.
Values may be sent and summed in bfloat16 or wider, within the bound.
No kernel may reach another device: no remote copies, remote signals or barrier semaphores. Data moves between devices by JAX's collectives and lax.ppermute only.
A program may use at most 128 MiB of HBM per device.

v0:
```python
from functools import partial

import jax
import jax.numpy as jnp
from jax import lax
from jax.experimental import pallas as pl
from jax.experimental.pallas import tpu as pltpu
from jax.sharding import PartitionSpec as P

HD = 104
PARTS_SIZE = 4
TOP = 2


EPSILON = 1e-06
ROOT_HALF = 0.7071067811865476
INV_ROOT_TWO_PI = 0.3989422804014327


def layer_norm(row_block, gain_vector):
    center = row_block - jnp.mean(row_block, axis=-1, keepdims=True)
    spread = jnp.mean(center * center, axis=-1, keepdims=True)
    return center * lax.rsqrt(spread + EPSILON) * gain_vector


def gelu_parts(preact):
    half_cdf = 0.5 * (1.0 + lax.erf(preact * ROOT_HALF))
    slope = half_cdf + preact * INV_ROOT_TWO_PI * jnp.exp(-0.5 * preact * preact)
    return preact * half_cdf, slope


def project_in(picture, first_gain, in_projection):
    normed = layer_norm(picture, first_gain).astype(jnp.bfloat16)
    return jnp.dot(normed, in_projection, preferred_element_type=jnp.float32).astype(jnp.bfloat16)


def attend(picture, joined, out_projection):
    seq_len = picture.shape[0]
    head_width = out_projection.shape[0]
    head_count = head_width // HD
    queries = joined[:, :head_width].reshape(seq_len, head_count, HD)
    key_rows = joined[:, head_width : 2 * head_width].reshape(seq_len, head_count, HD)
    value_rows = joined[:, 2 * head_width :].reshape(seq_len, head_count, HD)
    scores = jnp.einsum(
        "qhd,khd->hqk", queries, key_rows, preferred_element_type=jnp.float32
    ) * HD ** (-0.5)
    weights = jnp.exp(scores)
    attention = (weights / jnp.sum(weights, axis=-1, keepdims=True)).astype(jnp.bfloat16)
    context = jnp.einsum(
        "hqk,khd->qhd", attention, value_rows, preferred_element_type=jnp.float32
    ).astype(jnp.bfloat16)
    return picture + jnp.dot(
        context.reshape(seq_len, head_width), out_projection, preferred_element_type=jnp.float32
    )


def params():
    return pltpu.CompilerParams(vmem_limit_bytes=60 * 1024 * 1024)


SMALL = pl.CostEstimate(flops=1000, bytes_accessed=1000, transcendentals=0)
SCALARS = pl.BlockSpec(memory_space=pltpu.SMEM)
UNREAD = pl.BlockSpec(memory_space=pl.ANY)


def slot_table(spots_ref, slots_ref, images, sections, count):
    capacity = count // images
    rows = []
    for d in range(sections):
        columns = []
        for i in range(images):
            slots = slots_ref[spots_ref[i]][d : d + 1, :]
            lanes = lax.broadcasted_iota(jnp.int32, (count, slots.shape[1]), 0)
            hit = (lanes == slots + i * capacity) & (slots >= 0)
            columns.append(jnp.where(hit, 1.0, 0.0))
        rows.append(jnp.concatenate(columns, axis=1))
    return jnp.concatenate(rows, axis=0)


def pack_kernel(images, sections, inputs, *refs):
    spots_ref, slots_ref = refs[:2]
    dense = refs[2 : 2 + inputs]
    if inputs > 1:
        joined, blocks = refs[-1], refs[-1 - sections : -1]
        seq_len = dense[0].shape[0]
        for i in range(images):
            joined[i * seq_len : (i + 1) * seq_len, :] = dense[i][...]
    else:
        joined, blocks = dense[0], refs[-sections:]
    count = blocks[0].shape[0]
    table = slot_table(spots_ref, slots_ref, images, sections, count).astype(jnp.bfloat16)
    total = jnp.dot(table, joined[...], preferred_element_type=jnp.float32).astype(jnp.bfloat16)
    for d in range(sections):
        blocks[d][...] = total[d * count : (d + 1) * count, :]


def pack(spots, slots, dense, capacity, after=()):
    sections, seq_len = slots.shape[1:]
    width = dense[0].shape[1]
    inputs = len(dense)
    images = sum(block.shape[0] for block in dense) // seq_len
    count = images * capacity
    whole = pl.BlockSpec(memory_space=pltpu.VMEM)
    shapes = [jax.ShapeDtypeStruct((count, width), jnp.bfloat16)] * sections
    if inputs > 1:
        shapes.append(jax.ShapeDtypeStruct((images * seq_len, width), jnp.bfloat16))
    results = pl.pallas_call(
        partial(pack_kernel, images, sections, inputs),
        name="pack",
        in_specs=[SCALARS] + [whole] * (1 + inputs) + [UNREAD] * len(after),
        out_specs=[whole] * len(shapes),
        out_shape=shapes,
        compiler_params=params(),
        cost_estimate=SMALL,
    )(spots, slots, *dense, *after)
    return results[:sections], results[sections:]


EXTRA = 16


def unpack_kernel(images, sections, extra, scored, *refs):
    spots_ref, slots_ref = refs[:2]
    blocks = refs[2 : 2 + sections]
    addend = refs[2 + sections : 2 + sections + extra]
    partners = refs[2 + sections + extra : 2 + sections + extra + scored]
    joined = refs[-1]
    dense = refs[-1 - (images if extra or scored else 1) : -1]
    count = blocks[0].shape[0]
    seq_len = slots_ref.shape[2]
    for d in range(sections):
        joined[d * count : (d + 1) * count, :] = blocks[d][...]
    table = slot_table(spots_ref, slots_ref, images, sections, count)
    total = jnp.dot(
        table.T.astype(jnp.bfloat16), joined[...], preferred_element_type=jnp.float32
    )
    if scored:
        lines = []
        for d in range(sections):
            product = blocks[d][...].astype(jnp.float32) * partners[d][...].astype(jnp.float32)
            column = jnp.sum(product, axis=1, keepdims=True)
            lines.append(
                jnp.sum(table[d * count : (d + 1) * count, :] * column, axis=0, keepdims=True)
            )
        lines = jnp.concatenate(
            lines + [jnp.zeros((EXTRA - sections, lines[0].shape[1]), jnp.float32)], axis=0
        )
    if not (extra or scored):
        dense[0][...] = total.astype(jnp.bfloat16)
        return
    for i in range(images):
        part = total[i * seq_len : (i + 1) * seq_len, :]
        if extra:
            part = part + addend[0][i * seq_len : (i + 1) * seq_len, :].astype(jnp.float32)
        dense[i][:seq_len, :] = part.astype(jnp.bfloat16)
        if scored:
            dense[i][seq_len:, :] = jnp.zeros((EXTRA, total.shape[1]), jnp.bfloat16)
            dense[i][seq_len:, :seq_len] = lines[:, i * seq_len : (i + 1) * seq_len].astype(
                jnp.bfloat16
            )


def unpack(spots, slots, blocks, images, addend=(), partners=(), after=()):
    sections, seq_len = slots.shape[1:]
    count, width = blocks[0].shape
    whole = pl.BlockSpec(memory_space=pltpu.VMEM)
    inputs = sections + len(addend) + len(partners)
    height = seq_len + (EXTRA if partners else 0)
    parts = images if addend or partners else 1
    if parts == 1:
        height = images * seq_len
    return pl.pallas_call(
        partial(unpack_kernel, images, sections, len(addend), len(partners)),
        name="unpack",
        in_specs=[SCALARS] + [whole] * (1 + inputs) + [UNREAD] * len(after),
        out_specs=[whole] * parts,
        out_shape=[jax.ShapeDtypeStruct((height, width), jnp.bfloat16)] * parts,
        scratch_shapes=[pltpu.VMEM((sections * count, width), jnp.bfloat16)],
        compiler_params=params(),
        cost_estimate=SMALL,
    )(spots, slots, *blocks, *addend, *partners, *after)


def merge_kernel(sections, *refs):
    met = refs[sections]
    merged = refs[-sections:]
    count = merged[0].shape[0]
    for d in range(sections):
        total = refs[d][...].astype(jnp.float32)
        total = total + met[d * count : (d + 1) * count, :].astype(jnp.float32)
        merged[d][...] = total.astype(jnp.bfloat16)


def merge(blocks, met, after=()):
    sections = len(blocks)
    whole = pl.BlockSpec(memory_space=pltpu.VMEM)
    return pl.pallas_call(
        partial(merge_kernel, sections),
        name="merge",
        in_specs=[whole] * (sections + 1) + [UNREAD] * len(after),
        out_specs=[whole] * sections,
        out_shape=[jax.ShapeDtypeStruct(blocks[0].shape, jnp.bfloat16)] * sections,
        compiler_params=params(),
        cost_estimate=SMALL,
    )(*blocks, met, *after)


def expert_kernel(sections, images, split, unread, *refs):
    spots_ref, other_ref, router_ref = refs[:3]
    mixed_in = refs[3 : 3 + sections]
    pulls = 1 if split == 1 else sections
    grads_in = refs[3 + sections : 3 + sections + pulls]
    up_ref, down_ref = refs[3 + sections + pulls : 5 + sections + pulls]
    outs = refs[5 + sections + pulls + unread :]
    out_parts, grad_parts = outs[:split], outs[split : split + sections]
    mixed, grads, out_sum, grad_sum, gate_ref = outs[split + sections :]
    step, last = pl.program_id(0), pl.num_programs(0) - 1
    count = mixed_in[0].shape[0]
    total = count * sections
    capacity = count // images
    at_row = lax.broadcasted_iota(jnp.int32, (count, capacity), 0)
    at_slot = lax.broadcasted_iota(jnp.int32, (count, capacity), 1)

    @pl.when(step == 0)
    def _():
        others = []
        for d in range(sections):
            mixed[d * count : (d + 1) * count, :] = mixed_in[d][...]
            if split > 1:
                grads[d * count : (d + 1) * count, :] = grads_in[d][...]
            column = jnp.zeros((count, 1), jnp.int32)
            for i in range(images):
                ids = other_ref[spots_ref[images + 1 + d], pl.ds(spots_ref[i], 1), :]
                own = at_row == at_slot + i * capacity
                column = column + jnp.sum(jnp.where(own, ids, 0), axis=1, keepdims=True)
            others.append(column)
        if split == 1:
            grads[...] = grads_in[0][...]
        logits = jnp.dot(mixed[...], router_ref[...], preferred_element_type=jnp.float32)
        lanes = lax.broadcasted_iota(jnp.int32, logits.shape, 1)
        mine = jnp.sum(jnp.where(lanes == spots_ref[images], logits, 0.0), axis=1, keepdims=True)
        is_other = lanes == jnp.concatenate(others, axis=0)
        other = jnp.sum(jnp.where(is_other, logits, 0.0), axis=1, keepdims=True)
        gate_ref[...] = 1.0 / (1.0 + jnp.exp(other - mine))
        out_sum[...] = jnp.zeros_like(out_sum)
        grad_sum[...] = jnp.zeros_like(grad_sum)

    gate = gate_ref[...]
    preact = jnp.dot(mixed[...], up_ref[...], preferred_element_type=jnp.float32)
    pulled = gate * lax.dot_general(
        grads[...], down_ref[...], (((1,), (1,)), ((), ())), preferred_element_type=jnp.float32
    )
    hidden_wide, slope = gelu_parts(preact)
    hidden = hidden_wide.astype(jnp.bfloat16)
    hidden_grad = (pulled * slope).astype(jnp.bfloat16)
    out_sum[...] += jnp.dot(hidden, down_ref[...], preferred_element_type=jnp.float32)
    grad_sum[...] += lax.dot_general(
        hidden_grad, up_ref[...], (((1,), (1,)), ((), ())), preferred_element_type=jnp.float32
    )

    @pl.when(step == last)
    def _():
        size = total // split
        for part in range(split):
            rows = slice(part * size, (part + 1) * size)
            out_parts[part][...] = (out_sum[rows, :] * gate[rows, :]).astype(jnp.bfloat16)
        for d in range(sections):
            grad_parts[d][...] = grad_sum[d * count : (d + 1) * count, :].astype(jnp.bfloat16)


def expert_unit(spots, others, router, mixed_in, grads_in, up_local, down_local, split, after=()):
    sections = len(mixed_in)
    images = spots.shape[0] - 1 - sections
    count, width = mixed_in[0].shape
    total = count * sections
    hidden_units = up_local.shape[1]
    tile = 512
    assert hidden_units // tile >= 2

    def whole(shape):
        return pl.BlockSpec(shape, lambda f: (0,) * len(shape))

    block = whole((count, width))
    results = pl.pallas_call(
        partial(expert_kernel, sections, images, split, len(after)),
        name="expert",
        grid=(hidden_units // tile,),
        in_specs=[SCALARS, whole(others.shape), whole(router.shape)]
        + [block] * sections
        + [whole(block_in.shape) for block_in in grads_in]
        + [
            pl.BlockSpec((width, tile), lambda f: (0, f)),
            pl.BlockSpec((tile, width), lambda f: (f, 0)),
        ]
        + [UNREAD] * len(after),
        out_specs=[whole((total // split, width))] * split + [block] * sections,
        out_shape=[jax.ShapeDtypeStruct((total // split, width), jnp.bfloat16)] * split
        + [jax.ShapeDtypeStruct((count, width), jnp.bfloat16)] * sections,
        scratch_shapes=[
            pltpu.VMEM((total, width), jnp.bfloat16),
            pltpu.VMEM((total, width), jnp.bfloat16),
            pltpu.VMEM((total, width), jnp.float32),
            pltpu.VMEM((total, width), jnp.float32),
            pltpu.VMEM((total, 1), jnp.float32),
        ],
        compiler_params=params(),
        cost_estimate=SMALL,
    )(spots, others, router, *mixed_in, *grads_in, up_local, down_local, *after)
    return results[:split], results[split:]


def shards(
    tokens,
    route_ids,
    cotangent,
    first_gain,
    in_projection,
    out_projection,
    second_gain,
    router_weight,
    up_weight,
    down_weight,
):
    picture = tokens[0, 0].astype(jnp.float32)
    chosen = route_ids[0, 0]
    upstream = cotangent[0, 0]
    up_local = up_weight[0, 0]
    down_local = down_weight[0, 0]
    seq_len, width = picture.shape
    experts = router_weight.shape[1]
    sections = lax.axis_size("segment")
    members = lax.axis_size("expert")
    per_section = members // PARTS_SIZE
    capacity = 3 * seq_len // experts
    line = members // 2
    here = lax.axis_index("expert")
    section = lax.axis_index("segment")
    place, side = here // 2, here % 2
    group = here // PARTS_SIZE
    my_expert = section * per_section + group
    relative = section ^ jnp.arange(sections)
    experts_here = relative * per_section + group

    def along(value, steps):
        pairs = [(j, (j + 2 * steps) % members) for j in range(members)]
        return lax.ppermute(value, "expert", pairs)

    def across(value):
        return lax.ppermute(value, "expert", [(j, j ^ 1) for j in range(members)])

    def deal(blocks):
        moved = [blocks[0]]
        for d in range(1, sections):
            pairs = [(s, s ^ d) for s in range(sections)]
            moved.append(lax.ppermute(blocks[d], "segment", pairs))
        return moved

    def deal_small(value):
        return lax.all_to_all(
            jnp.take(value, relative, axis=0), "segment", split_axis=0, concat_axis=0, tiled=True
        )

    half = line // 2
    chunks = [list(range(line - 1, half - 1, -1)), list(range(half - 1, -1, -1))]

    expert_list = jnp.arange(experts)
    hits = jnp.any(chosen.T[None] == expert_list[:, None, None], axis=1)
    tokens_before = jnp.arange(seq_len)[:, None] < jnp.arange(seq_len)[None, :]
    own_slots = jnp.dot(
        hits.astype(jnp.bfloat16),
        tokens_before.astype(jnp.bfloat16),
        preferred_element_type=jnp.float32,
    ).astype(jnp.int32)
    own_slots = jnp.where(hits, own_slots, -1)
    others = jnp.sum(chosen, axis=1)[None, :] - expert_list[:, None]
    at_slot = own_slots[:, None, :] == jnp.arange(capacity)[None, :, None]
    own_others = jnp.sum(jnp.where(at_slot, others[:, None, :], 0), axis=2)
    wide = jnp.concatenate([own_slots, own_others], axis=1)
    wide = jnp.take(wide.reshape(sections, per_section, -1), relative, axis=0).transpose(1, 0, 2)
    wide = jnp.broadcast_to(
        wide[:, None], (per_section, PARTS_SIZE) + wide.shape[1:]
    ).reshape(members, -1)
    lane = lax.all_to_all(wide, "expert", split_axis=0, concat_axis=0, tiled=True).reshape(
        members, sections, seq_len + capacity
    )
    slots = lane[:, :, :seq_len]
    slot_others = deal_small(lane[:, :, seq_len:].transpose(1, 0, 2))

    def spots_of(index, far):
        places = (place - jnp.array(chunks[index])) % line
        side_of = (1 - side) if far else side
        return jnp.concatenate(
            [2 * places + side_of, my_expert.reshape(1), relative]
        ).astype(jnp.int32)

    spots = {(index, far): spots_of(index, far) for index in (0, 1) for far in (0, 1)}

    cot_dense = {0: upstream, 1: along(upstream, 1)}
    slots, late_upstream = lax.optimization_barrier((slots, upstream))
    for step in range(2, line):
        cot_dense[step] = along(late_upstream, step)

    def cot_pack(index):
        dense = [cot_dense[step] for step in chunks[index]]
        return pack(spots[index, 0], slots, dense, capacity)[0]

    joined, project_back = jax.vjp(
        partial(project_in, first_gain=first_gain, in_projection=in_projection), picture
    )
    cot_packed, cot_rows = {}, {}
    cot_packed[1] = cot_pack(1)
    joined, cot_packed[1] = lax.optimization_barrier((joined, cot_packed[1]))
    cot_rows[1, 0] = deal(cot_packed[1])
    residual, attend_back = jax.vjp(partial(attend, out_projection=out_projection), picture, joined)
    residual, cot_rows[1, 0], slot_others = lax.optimization_barrier(
        (residual, cot_rows[1, 0], slot_others)
    )
    normed, norm_back = jax.vjp(partial(layer_norm, gain_vector=second_gain), residual)
    mixed = normed.astype(jnp.bfloat16)
    own_logits = jnp.dot(mixed, router_weight, preferred_element_type=jnp.float32)

    mixed_dense = {0: mixed}
    for step in range(1, line):
        mixed_dense[step] = along(mixed, step)

    cot_rows[1, 1] = [across(jnp.concatenate(cot_rows[1, 0], axis=0))]
    cot_packed[0] = cot_pack(0)
    cot_rows[0, 0] = deal(cot_packed[0])

    mixed_rows, far_dense = {}, {}

    def mixed_pack(index, after):
        dense = [mixed_dense[step] for step in chunks[index]]
        blocks, joined_dense = pack(spots[index, 0], slots, dense, capacity, after)
        far_dense[index] = across(joined_dense[0])
        mixed_rows[index, 0] = deal(blocks)
        return (blocks[0],)

    def far_pack(index, after):
        blocks, _ = pack(spots[index, 1], slots, [far_dense[index]], capacity, after)
        mixed_rows[index, 1] = deal(blocks)
        return (blocks[0],)

    outs, grads = {}, {}

    def unit(index, far, after):
        outs[index, far], grads[index, far] = expert_unit(
            spots[index, far],
            slot_others,
            router_weight,
            mixed_rows[index, far],
            cot_rows[index, far],
            up_local,
            down_local,
            1 if far else sections,
            after,
        )
        done = (grads[index, far][0],)
        grads[index, far] = deal(grads[index, far])
        return done

    done = mixed_pack(1, (cot_packed[0][0],))
    done = mixed_pack(0, done + tuple(cot_rows[1, 1]))
    cot_rows[0, 1] = [across(jnp.concatenate(cot_rows[0, 0], axis=0))]
    done = far_pack(1, done)
    done = unit(1, 0, done)
    done = far_pack(0, done)
    done = unit(0, 0, done)
    done = unit(1, 1, done + tuple(grads[1, 0][1:]))
    met = {1: across(outs[1, 1][0])}
    done = unit(0, 1, done + tuple(grads[0, 0][1:]))
    met[0] = across(outs[0, 1][0])

    grad_far, out_back, out_dense, grad_dense = {}, {}, {}, {}
    for index in (1, 0):
        count = len(chunks[index])
        grad_far[index] = unpack(spots[index, 1], slots, grads[index, 1], count, after=done)[0]
        done = (grad_far[index],)
        grad_far[index] = across(grad_far[index])
        merged = merge(outs[index, 0], met[index], done)
        done = (merged[0],)
        out_back[index] = deal(merged)
    for index in (1, 0):
        chunk = chunks[index]
        count = len(chunk)
        out_block = unpack(
            spots[index, 0], slots, out_back[index], count, (), cot_packed[index], done
        )
        done = (out_block[0],)
        grad_block = unpack(
            spots[index, 0], slots, grads[index, 0], count, (grad_far[index],), (), done
        )
        done = (grad_block[0],)
        for spot, step in enumerate(chunk):
            part_out, part_grad = out_block[spot], grad_block[spot]
            out_dense[step] = along(part_out, -step) if step else part_out
            grad_dense[step] = along(part_grad, -step) if step else part_grad
        done += tuple(out_dense[step] for step in chunk if step)

    expert_total = sum(out_dense[step][:seq_len].astype(jnp.float32) for step in range(line))
    input_total = sum(grad_dense[step].astype(jnp.float32) for step in range(line))
    layer_out = (residual + expert_total).astype(jnp.bfloat16)

    named = chosen[:, :, None] == expert_list
    score_lines = jnp.zeros((per_section, sections, seq_len), jnp.float32)
    for step in range(line):
        sender = 2 * ((place + step) % line) // PARTS_SIZE
        lines = out_dense[step][seq_len : seq_len + sections, :seq_len].astype(jnp.float32)
        score_lines += jnp.where((jnp.arange(per_section) == sender)[:, None, None], lines, 0.0)
    token_scores = (
        jnp.take(score_lines, relative, axis=1).transpose(1, 0, 2).reshape(experts, seq_len).T
    )
    picked_logit = jnp.sum(jnp.where(named, own_logits[:, None, :], 0.0), axis=2)
    gate_values = 1.0 / (1.0 + jnp.exp(picked_logit[:, ::-1] - picked_logit))
    gate_spread = jnp.sum(jnp.where(named, gate_values[:, :, None], 0.0), axis=1)
    spread_grad = token_scores - gate_spread * jnp.sum(token_scores, axis=1, keepdims=True)
    mixed_grad = input_total + jnp.einsum(
        "se,de->sd", spread_grad, router_weight.astype(jnp.float32), precision=lax.Precision.HIGHEST
    )
    residual_grad = upstream.astype(jnp.float32) + norm_back(mixed_grad)[0]
    picture_grad, joined_grad = attend_back(residual_grad)
    input_grad = (picture_grad + project_back(joined_grad)[0]).astype(jnp.bfloat16)
    return (layer_out[None, None], input_grad[None, None])


def solution(mesh):
    placed = (
        P("segment", "expert", None, None),
        P("segment", "expert", None, None),
        P("segment", "expert", None, None),
        P(),
        P(),
        P(),
        P(),
        P(),
        P("segment", "expert", None, None),
        P("segment", "expert", None, None),
    )
    return jax.shard_map(
        shards,
        mesh=mesh,
        in_specs=placed,
        out_specs=(P("segment", "expert", None, None), P("segment", "expert", None, None)),
        check_vma=False,
    )
```

profile of v0, /device:TPU:0, one launch (start us, length us, event | category | flops | bytes accessed | tf_op | source)
XLA Modules:
  0.0 373.0 jit_solution(11648162713653867084)
XLA Ops:
  4.0 7.3 %all-to-all-start = ((s32[8,1,704]{2,1,0:T(1,128)}), s32[8,1,704]{2,1,0:T(1,128)S(1)}, u32[]{:S(2)}, u32[]{:S(2)}) async-start(s32[8,1,704]{2,1,0:T(1,128)} %all_to_all.9), calls=%async_computation | async-start | bytes 49152 | tf_op jit(solution)/shard_map/all_to_all | solution.py:383
  16.5 6.8 %convolution_convert_fusion = bf16[128,2496]{0,1:T(8,128)(2,1)} fusion(bf16[1664,2496]{0,1:T(8,128)(2,1)} %param.18, bf16[1,1,128,1664]{3,2,1,0:T(8,128)(2,1)} %param.14, f32[1664]{0:T(1024)} %param.17, f32[128]{0:T(128)S(1)} %fusion.36, f32[128]{0:T(128)S(1)} %broadcast_multiply_fusion.1), kind=kOutput, calls=%fused_computation.3 | convolution fusion | flops 1064640512 | bytes 9379328 | tf_op jit(solution)/shard_map/jvp()/dot_general | solution.py:34
  26.5 3.2 all-to-all-start.1
  35.4 3.0 pack.6
  44.3 6.1 %collective-permute-done.2.refs_9_ = bf16[96,1664]{1,0:T(8,128)(2,1)} collective-permute-done((bf16[96,1664]{1,0:T(8,128)(2,1)}, bf16[96,1664]{1,0:T(8,128)(2,1)}, u32[]{:S(2)}, u32[]{:S(2)}) %collective-permute-start.2) | collective-permute-done | bytes 319520 | tf_op jit(solution)/shard_map/ppermute | solution.py:355
  50.5 5.9 %collective-permute-done.3.refs_10_ = bf16[96,1664]{1,0:T(8,128)(2,1)} collective-permute-done((bf16[96,1664]{1,0:T(8,128)(2,1)}, bf16[96,1664]{1,0:T(8,128)(2,1)}, u32[]{:S(2)}, u32[]{:S(2)}) %collective-permute-start.3) | collective-permute-done | bytes 319520 | tf_op jit(solution)/shard_map/ppermute | solution.py:355
  66.8 3.0 pack.7
  69.8 8.2 %collective-permute-done.4.refs_2_ = bf16[128,1664]{1,0:T(8,128)(2,1)} collective-permute-done((bf16[128,1664]{1,0:T(8,128)(2,1)S(1)}, bf16[128,1664]{1,0:T(8,128)(2,1)}, u32[]{:S(2)}, u32[]{:S(2)}) %collective-permute-start.4) | collective-permute-done | bytes 426016 | tf_op jit(solution)/shard_map/ppermute | solution.py:346
  78.0 3.0 pack.8
  83.9 11.5 %collective-permute-done.12.refs_3_ = bf16[128,1664]{1,0:T(8,128)(2,1)} collective-permute-done((bf16[128,1664]{1,0:T(8,128)(2,1)S(1)}, bf16[128,1664]{1,0:T(8,128)(2,1)}, u32[]{:S(2)}, u32[]{:S(2)}) %collective-permute-start.12) | collective-permute-done | bytes 426016 | tf_op jit(solution)/shard_map/ppermute | solution.py:346
  95.7 4.2 %collective-permute-done.11.refs_2_ = bf16[128,1664]{1,0:T(8,128)(2,1)} collective-permute-done((bf16[128,1664]{1,0:T(8,128)(2,1)}, bf16[128,1664]{1,0:T(8,128)(2,1)}, u32[]{:S(2)}, u32[]{:S(2)}) %collective-permute-start.11) | collective-permute-done | bytes 426016 | tf_op jit(solution)/shard_map/ppermute | solution.py:346
  101.8 3.0 pack.9
  119.4 11.8 %expert.4 = (bf16[96,1664]{1,0:T(8,128)(2,1)}, bf16[96,1664]{1,0:T(8,128)(2,1)}, bf16[96,1664]{1,0:T(8,128)(2,1)}, bf16[96,1664]{1,0:T(8,128)(2,1)}, bf16[96,166...) custom-call(s32[7]{0:T(128)} %add_add_fusion.4.refs_0_, ...), custom_call_target="tpu_custom_call" | custom-call | flops 1000 | bytes 1000 | tf_op jit(solution)/shard_map/expert/pallas_call | solution.py:284
  134.6 8.4 %collective-permute-done.25.refs_12_.refs_4_ = bf16[96,1664]{1,0:T(8,128)(2,1)S(1)} collective-permute-done((bf16[96,1664]{1,0:T(8,128)(2,1)}, bf16[96,1664]{1,0:T(8,128)(2,1)S(1)}, u32[]{:S(2)}, u32[]{:S(2)}) %collective-permute-start.25) | collective-permute-done | bytes 319520 | tf_op jit(solution)/shard_map/ppermute | solution.py:355
  146.5 11.8 %expert.5 = (bf16[96,1664]{1,0:T(8,128)(2,1)}, bf16[96,1664]{1,0:T(8,128)(2,1)}, bf16[96,1664]{1,0:T(8,128)(2,1)}, bf16[96,1664]{1,0:T(8,128)(2,1)}, bf16[96,166...) custom-call(s32[7]{0:T(128)} %get-tuple-element.180.refs_0_, ...), custom_call_target="tpu_custom_call" | custom-call | flops 1000 | bytes 1000 | tf_op jit(solution)/shard_map/expert/pallas_call | solution.py:284
  162.0 12.0 %expert.6 = (bf16[384,1664]{1,0:T(8,128)(2,1)}, bf16[96,1664]{1,0:T(8,128)(2,1)}, bf16[96,1664]{1,0:T(8,128)(2,1)}, bf16[96,1664]{1,0:T(8,128)(2,1)}, bf16[96,1664]{1,0:T(8,128)(2,1)}) custom-call(s32[7]{0:T(128)} %get-tuple-element.178.refs_0_, s32[4,8,48]{2,1,0:T(8,128)} %reshape.209.refs_1_, bf16[1664,8]{1,0:T(8,128)(2,1)} %copy.58.refs_2_, ...), custom_call_target="tpu_custom_call" | custom-call | flops 1000 | bytes 1000 | tf_op jit(solution)/shard_map/expert/pallas_call | solution.py:284
  177.3 7.0 %collective-permute-done.37.refs_13_.refs_5_ = bf16[96,1664]{1,0:T(8,128)(2,1)} collective-permute-done((bf16[96,1664]{1,0:T(8,128)(2,1)}, bf16[96,1664]{1,0:T(8,128)(2,1)}, u32[]{:S(2)}, u32[]{:S(2)}) %collective-permute-start.37) | collective-permute-done | bytes 319520 | tf_op jit(solution)/shard_map/ppermute | solution.py:355
  184.3 8.1 %collective-permute-done.32.refs_5_ = bf16[96,1664]{1,0:T(8,128)(2,1)} collective-permute-done((bf16[96,1664]{1,0:T(8,128)(2,1)}, bf16[96,1664]{1,0:T(8,128)(2,1)}, u32[]{:S(2)}, u32[]{:S(2)}) %collective-permute-start.32) | collective-permute-done | bytes 319520 | tf_op jit(solution)/shard_map/ppermute | solution.py:355
  192.4 5.6 %collective-permute-done.33.refs_6_ = bf16[96,1664]{1,0:T(8,128)(2,1)} collective-permute-done((bf16[96,1664]{1,0:T(8,128)(2,1)}, bf16[96,1664]{1,0:T(8,128)(2,1)}, u32[]{:S(2)}, u32[]{:S(2)}) %collective-permute-start.33) | collective-permute-done | bytes 319520 | tf_op jit(solution)/shard_map/ppermute | solution.py:355
  198.0 11.8 %expert.7 = (bf16[384,1664]{1,0:T(8,128)(2,1)}, bf16[96,1664]{1,0:T(8,128)(2,1)}, bf16[96,1664]{1,0:T(8,128)(2,1)}, bf16[96,1664]{1,0:T(8,128)(2,1)}, bf16[96,1664]{1,0:T(8,128)(2,1)}) custom-call(s32[7]{0:T(128)} %get-tuple-element.179.refs_0_, s32[4,8,48]{2,1,0:T(8,128)} %reshape.209.refs_1_, bf16[1664,8]{1,0:T(8,128)(2,1)} %copy.58.refs_2_, ...), custom_call_target="tpu_custom_call" | custom-call | flops 1000 | bytes 1000 | tf_op jit(solution)/shard_map/expert/pallas_call | solution.py:284
  213.7 8.6 %collective-permute-done.29.refs_4_ = bf16[96,1664]{1,0:T(8,128)(2,1)} collective-permute-done((bf16[96,1664]{1,0:T(8,128)(2,1)}, bf16[96,1664]{1,0:T(8,128)(2,1)}, u32[]{:S(2)}, u32[]{:S(2)}) %collective-permute-start.29) | collective-permute-done | bytes 319520 | tf_op jit(solution)/shard_map/ppermute | solution.py:355
  222.9 4.5 %collective-permute-done.30.refs_5_ = bf16[96,1664]{1,0:T(8,128)(2,1)} collective-permute-done((bf16[96,1664]{1,0:T(8,128)(2,1)}, bf16[96,1664]{1,0:T(8,128)(2,1)}, u32[]{:S(2)}, u32[]{:S(2)}) %collective-permute-start.30) | collective-permute-done | bytes 319520 | tf_op jit(solution)/shard_map/ppermute | solution.py:355
  250.4 4.4 %collective-permute-done.40.refs_5_ = bf16[96,1664]{1,0:T(8,128)(2,1)} collective-permute-done((bf16[96,1664]{1,0:T(8,128)(2,1)}, bf16[96,1664]{1,0:T(8,128)(2,1)}, u32[]{:S(2)}, u32[]{:S(2)}) %collective-permute-start.40) | collective-permute-done | bytes 319520 | tf_op jit(solution)/shard_map/ppermute | solution.py:355
  254.8 3.5 unpack.8
  258.3 11.0 %collective-permute-start.45 = (bf16[144,1664]{1,0:T(8,128)(2,1)}, bf16[144,1664]{1,0:T(8,128)(2,1)}, u32[]{:S(2)}, u32[]{:S(2)}) collective-permute-start(bf16[144,1664]{1,0:T(8,128)(2,1)} %get-tuple-element.154.refs_7_), channel_id=1, source_target_pairs={{0,24},{4,28},{8,0},{12,4},{16,8},{20,12},{24,16},{28,20},{1,25},{... | collective-permute-start | bytes 1437704 | tf_op jit(solution)/shard_map/ppermute | solution.py:346
  275.9 3.2 unpack.9
  279.1 2.9 collective-permute-done.47.refs_4_
  282.0 5.1 %collective-permute-done.48.refs_5_ = bf16[96,1664]{1,0:T(8,128)(2,1)} collective-permute-done((bf16[96,1664]{1,0:T(8,128)(2,1)}, bf16[96,1664]{1,0:T(8,128)(2,1)}, u32[]{:S(2)}, u32[]{:S(2)}) %collective-permute-start.48) | collective-permute-done | bytes 319520 | tf_op jit(solution)/shard_map/ppermute | solution.py:355
  287.1 3.5 unpack.10
  294.1 3.1 unpack.11
  300.1 41.6 %collective-permute-done.50 = bf16[144,1664]{1,0:T(8,128)(2,1)S(1)} collective-permute-done((bf16[144,1664]{1,0:T(8,128)(2,1)}, bf16[144,1664]{1,0:T(8,128)(2,1)S(1)}, u32[]{:S(2)}, u32[]{:S(2)}) %collective-permute-start.50) | collective-permute-done | bytes 479264 | tf_op jit(solution)/shard_map/ppermute | solution.py:346
  344.7 15.4 %collective-permute-done.54 = bf16[128,1664]{1,0:T(8,128)(2,1)} collective-permute-done((bf16[128,1664]{1,0:T(8,128)(2,1)}, bf16[128,1664]{1,0:T(8,128)(2,1)}, u32[]{:S(2)}, u32[]{:S(2)}) %collective-permute-start.54) | collective-permute-done | bytes 426016 | tf_op jit(solution)/shard_map/ppermute | solution.py:346
  (291 shorter events, 122.7 us)
Async XLA Ops:
  4.0 21.0 %all-to-all-start = ((s32[8,1,704]{2,1,0:T(1,128)}), s32[8,1,704]{2,1,0:T(1,128)S(1)}, u32[]{:S(2)}, u32[]{:S(2)}) async-start(s32[8,1,704]{2,1,0:T(1,128)} %all_to_all.9), calls=%async_computation | async-start | bytes 49152 | tf_op jit(solution)/shard_map/all_to_all | solution.py:383
  11.3 24.1 %collective-permute-start = (bf16[128,1664]{1,0:T(8,128)(2,1)}, bf16[128,1664]{1,0:T(8,128)(2,1)}, u32[]{:S(2)}, u32[]{:S(2)}) collective-permute-start(bf16[128,1664]{1,0:T(8,128)(2,1)} %bitcast.6.refs_3_), channel_id=1, source_target_pairs={{0,8},{4,12},{8,16},{12,20},{16,24},{20,28},{24,0},{28,4},{1,9},{5... | collective-permute-start | bytes 1277960 | tf_op jit(solution)/shard_map/ppermute | solution.py:346
  31.0 35.8 %collective-permute-start.6 = (bf16[128,1664]{1,0:T(8,128)(2,1)}, bf16[128,1664]{1,0:T(8,128)(2,1)}, u32[]{:S(2)}, u32[]{:S(2)}) collective-permute-start(bf16[128,1664]{1,0:T(8,128)(2,1)} %bitcast.6.refs_3_), channel_id=1, source_target_pairs={{0,16},{4,20},{8,24},{12,28},{16,0},{20,4},{24,8},{28,12},{1,17},{... | collective-permute-start | bytes 1277960 | tf_op jit(solution)/shard_map/ppermute | solution.py:346
  31.6 35.1 %collective-permute-start.5 = (bf16[128,1664]{1,0:T(8,128)(2,1)}, bf16[128,1664]{1,0:T(8,128)(2,1)}, u32[]{:S(2)}, u32[]{:S(2)}) collective-permute-start(bf16[128,1664]{1,0:T(8,128)(2,1)} %bitcast.6.refs_3_), channel_id=1, source_target_pairs={{0,24},{4,28},{8,0},{12,4},{16,8},{20,12},{24,16},{28,20},{1,25},{... | collective-permute-start | bytes 1277960 | tf_op jit(solution)/shard_map/ppermute | solution.py:346
  61.5 38.4 %collective-permute-start.13 = (bf16[384,1664]{1,0:T(8,128)(2,1)}, bf16[384,1664]{1,0:T(8,128)(2,1)}, u32[]{:S(2)}, u32[]{:S(2)}) collective-permute-start(bf16[384,1664]{1,0:T(8,128)(2,1)} %pad_maximum_fusion), channel_id=1, source_target_pairs={{0,4},{4,0},{8,12},{12,8},{16,20},{20,16},{24,28},{28,24},{1,5},{5... | collective-permute-start | bytes 3833864 | tf_op jit(solution)/shard_map/ppermute | solution.py:349
  63.7 31.6 %collective-permute-start.12 = (bf16[128,1664]{1,0:T(8,128)(2,1)S(1)}, bf16[128,1664]{1,0:T(8,128)(2,1)}, u32[]{:S(2)}, u32[]{:S(2)}) collective-permute-start(bf16[128,1664]{1,0:T(8,128)(2,1)S(1)} %multiply_convert_fusion.refs_3_), channel_id=1, source_target_pairs={{0,16},{4,20},{8,24},{12,28},{16,0},{20,4},{24,8},{28,12},{1,17},{... | collective-permute-start | bytes 1277960 | tf_op jit(solution)/shard_map/ppermute | solution.py:346
  81.0 31.5 %collective-permute-start.10 = (bf16[256,1664]{1,0:T(8,128)(2,1)}, bf16[256,1664]{1,0:T(8,128)(2,1)}, u32[]{:S(2)}, u32[]{:S(2)}) collective-permute-start(bf16[256,1664]{1,0:T(8,128)(2,1)} %get-tuple-element.105), channel_id=1, source_target_pairs={{0,4},{4,0},{8,12},{12,8},{16,20},{20,16},{24,28},{28,24},{1,5},{5... | collective-permute-start | bytes 2555912 | tf_op jit(solution)/shard_map/ppermute | solution.py:349
  81.5 18.4 %collective-permute-start.11 = (bf16[128,1664]{1,0:T(8,128)(2,1)}, bf16[128,1664]{1,0:T(8,128)(2,1)}, u32[]{:S(2)}, u32[]{:S(2)}) collective-permute-start(bf16[128,1664]{1,0:T(8,128)(2,1)} %copy-done.5), channel_id=1, source_target_pairs={{0,24},{4,28},{8,0},{12,4},{16,8},{20,12},{24,16},{28,20},{1,25},{... | collective-permute-start | bytes 1277960 | tf_op jit(solution)/shard_map/ppermute | solution.py:346
  82.1 22.7 %collective-permute-start.21 = (bf16[96,1664]{1,0:T(8,128)(2,1)}, bf16[96,1664]{1,0:T(8,128)(2,1)}, u32[]{:S(2)}, u32[]{:S(2)}) collective-permute-start(bf16[96,1664]{1,0:T(8,128)(2,1)} %get-tuple-element.119.refs_8_), channel_id=1, source_target_pairs={{0,2},{1,3},{2,0},{3,1},{4,6},{5,7},{6,4},{7,5},{8,10},{9,11},{10,... | collective-permute-start | bytes 958472 | tf_op jit(solution)/shard_map/ppermute | solution.py:355
  105.4 38.4 %collective-permute-start.23 = (bf16[256,1664]{1,0:T(8,128)(2,1)}, bf16[256,1664]{1,0:T(8,128)(2,1)}, u32[]{:S(2)}, u32[]{:S(2)}) collective-permute-start(bf16[256,1664]{1,0:T(8,128)(2,1)} %get-tuple-element.121), channel_id=1, source_target_pairs={{0,4},{4,0},{8,12},{12,8},{16,20},{20,16},{24,28},{28,24},{1,5},{5... | collective-permute-start | bytes 2555912 | tf_op jit(solution)/shard_map/ppermute | solution.py:349
  108.7 66.8 %collective-permute-start.34 = (bf16[384,1664]{1,0:T(8,128)(2,1)}, bf16[384,1664]{1,0:T(8,128)(2,1)}, u32[]{:S(2)}, u32[]{:S(2)}) collective-permute-start(bf16[384,1664]{1,0:T(8,128)(2,1)} %pad_maximum_fusion.1), channel_id=1, source_target_pairs={{0,4},{4,0},{8,12},{12,8},{16,20},{20,16},{24,28},{28,24},{1,5},{5... | collective-permute-start | bytes 3833864 | tf_op jit(solution)/shard_map/ppermute | solution.py:349
  112.3 18.9 %collective-permute-start.17 = (bf16[96,1664]{1,0:T(8,128)(2,1)}, bf16[96,1664]{1,0:T(8,128)(2,1)}, u32[]{:S(2)}, u32[]{:S(2)}) collective-permute-start(bf16[96,1664]{1,0:T(8,128)(2,1)} %get-tuple-element.115), channel_id=1, source_target_pairs={{0,1},{1,0},{2,3},{3,2},{4,5},{5,4},{6,7},{7,6},{8,9},{9,8},{10,11... | collective-permute-start | bytes 958472 | tf_op jit(solution)/shard_map/ppermute | solution.py:355
  112.5 20.0 %collective-permute-start.18 = (bf16[96,1664]{1,0:T(8,128)(2,1)}, bf16[96,1664]{1,0:T(8,128)(2,1)}, u32[]{:S(2)}, u32[]{:S(2)}) collective-permute-start(bf16[96,1664]{1,0:T(8,128)(2,1)} %get-tuple-element.116), channel_id=1, source_target_pairs={{0,2},{1,3},{2,0},{3,1},{4,6},{5,7},{6,4},{7,5},{8,10},{9,11},{10,... | collective-permute-start | bytes 958472 | tf_op jit(solution)/shard_map/ppermute | solution.py:355
  133.2 25.1 %collective-permute-start.26 = (bf16[96,1664]{1,0:T(8,128)(2,1)}, bf16[96,1664]{1,0:T(8,128)(2,1)}, u32[]{:S(2)}, u32[]{:S(2)}) collective-permute-start(bf16[96,1664]{1,0:T(8,128)(2,1)} %get-tuple-element.127), channel_id=1, source_target_pairs={{0,3},{1,2},{2,1},{3,0},{4,7},{5,6},{6,5},{7,4},{8,11},{9,10},{10,... | collective-permute-start | bytes 958472 | tf_op jit(solution)/shard_map/ppermute | solution.py:355
  133.9 25.9 %collective-permute-start.14 = (bf16[96,1664]{1,0:T(8,128)(2,1)}, bf16[96,1664]{1,0:T(8,128)(2,1)}, u32[]{:S(2)}, u32[]{:S(2)}) collective-permute-start(bf16[96,1664]{1,0:T(8,128)(2,1)} %get-tuple-element.112), channel_id=1, source_target_pairs={{0,1},{1,0},{2,3},{3,2},{4,5},{5,4},{6,7},{7,6},{8,9},{9,8},{10,11... | collective-permute-start | bytes 958472 | tf_op jit(solution)/shard_map/ppermute | solution.py:355
  143.1 17.4 %collective-permute-start.15 = (bf16[96,1664]{1,0:T(8,128)(2,1)}, bf16[96,1664]{1,0:T(8,128)(2,1)}, u32[]{:S(2)}, u32[]{:S(2)}) collective-permute-start(bf16[96,1664]{1,0:T(8,128)(2,1)} %get-tuple-element.113), channel_id=1, source_target_pairs={{0,2},{1,3},{2,0},{3,1},{4,6},{5,7},{6,4},{7,5},{8,10},{9,11},{10,... | collective-permute-start | bytes 958472 | tf_op jit(solution)/shard_map/ppermute | solution.py:355
  143.8 18.2 %collective-permute-start.16 = (bf16[96,1664]{1,0:T(8,128)(2,1)}, bf16[96,1664]{1,0:T(8,128)(2,1)}, u32[]{:S(2)}, u32[]{:S(2)}) collective-permute-start(bf16[96,1664]{1,0:T(8,128)(2,1)} %get-tuple-element.114), channel_id=1, source_target_pairs={{0,3},{1,2},{2,1},{3,0},{4,7},{5,6},{6,5},{7,4},{8,11},{9,10},{10,... | collective-permute-start | bytes 958472 | tf_op jit(solution)/shard_map/ppermute | solution.py:355
  158.3 17.2 %collective-permute-start.35 = (bf16[96,1664]{1,0:T(8,128)(2,1)}, bf16[96,1664]{1,0:T(8,128)(2,1)S(1)}, u32[]{:S(2)}, u32[]{:S(2)}) collective-permute-start(bf16[96,1664]{1,0:T(8,128)(2,1)} %get-tuple-element.136), channel_id=1, source_target_pairs={{0,1},{1,0},{2,3},{3,2},{4,5},{5,4},{6,7},{7,6},{8,9},{9,8},{10,11... | collective-permute-start | bytes 958472 | tf_op jit(solution)/shard_map/ppermute | solution.py:355
  159.8 17.2 %collective-permute-start.36 = (bf16[96,1664]{1,0:T(8,128)(2,1)}, bf16[96,1664]{1,0:T(8,128)(2,1)S(1)}, u32[]{:S(2)}, u32[]{:S(2)}) collective-permute-start(bf16[96,1664]{1,0:T(8,128)(2,1)} %get-tuple-element.137), channel_id=1, source_target_pairs={{0,2},{1,3},{2,0},{3,1},{4,6},{5,7},{6,4},{7,5},{8,10},{9,11},{10,... | collective-permute-start | bytes 958472 | tf_op jit(solution)/shard_map/ppermute | solution.py:355
  174.0 58.4 %collective-permute-start.27 = (bf16[384,1664]{1,0:T(8,128)(2,1)}, bf16[384,1664]{1,0:T(8,128)(2,1)}, u32[]{:S(2)}, u32[]{:S(2)}) collective-permute-start(bf16[384,1664]{1,0:T(8,128)(2,1)} %get-tuple-element.128), channel_id=1, source_target_pairs={{0,4},{4,0},{8,12},{12,8},{16,20},{20,16},{24,28},{28,24},{1,5},{5... | collective-permute-start | bytes 3833864 | tf_op jit(solution)/shard_map/ppermute | solution.py:349
  175.5 16.9 %collective-permute-start.32 = (bf16[96,1664]{1,0:T(8,128)(2,1)}, bf16[96,1664]{1,0:T(8,128)(2,1)}, u32[]{:S(2)}, u32[]{:S(2)}) collective-permute-start(bf16[96,1664]{1,0:T(8,128)(2,1)} %get-tuple-element.134), channel_id=1, source_target_pairs={{0,2},{1,3},{2,0},{3,1},{4,6},{5,7},{6,4},{7,5},{8,10},{9,11},{10,... | collective-permute-start | bytes 958472 | tf_op jit(solution)/shard_map/ppermute | solution.py:355
  177.0 21.0 %collective-permute-start.33 = (bf16[96,1664]{1,0:T(8,128)(2,1)}, bf16[96,1664]{1,0:T(8,128)(2,1)}, u32[]{:S(2)}, u32[]{:S(2)}) collective-permute-start(bf16[96,1664]{1,0:T(8,128)(2,1)} %get-tuple-element.135), channel_id=1, source_target_pairs={{0,3},{1,2},{2,1},{3,0},{4,7},{5,6},{6,5},{7,4},{8,11},{9,10},{10,... | collective-permute-start | bytes 958472 | tf_op jit(solution)/shard_map/ppermute | solution.py:355
  209.8 37.7 %collective-permute-start.41 = (bf16[384,1664]{1,0:T(8,128)(2,1)}, bf16[384,1664]{1,0:T(8,128)(2,1)}, u32[]{:S(2)}, u32[]{:S(2)}) collective-permute-start(bf16[384,1664]{1,0:T(8,128)(2,1)} %get-tuple-element.148), channel_id=1, source_target_pairs={{0,4},{4,0},{8,12},{12,8},{16,20},{20,16},{24,28},{28,24},{1,5},{5... | collective-permute-start | bytes 3833864 | tf_op jit(solution)/shard_map/ppermute | solution.py:349
  213.0 23.5 %collective-permute-start.42 = (bf16[96,1664]{1,0:T(8,128)(2,1)}, bf16[96,1664]{1,0:T(8,128)(2,1)S(1)}, u32[]{:S(2)}, u32[]{:S(2)}) collective-permute-start(bf16[96,1664]{1,0:T(8,128)(2,1)} %get-tuple-element.149), channel_id=1, source_target_pairs={{0,1},{1,0},{2,3},{3,2},{4,5},{5,4},{6,7},{7,6},{8,9},{9,8},{10,11... | collective-permute-start | bytes 958472 | tf_op jit(solution)/shard_map/ppermute | solution.py:355
  232.4 39.7 %collective-permute-start.49 = (bf16[256,1664]{1,0:T(8,128)(2,1)}, bf16[256,1664]{1,0:T(8,128)(2,1)}, u32[]{:S(2)}, u32[]{:S(2)}) collective-permute-start(bf16[256,1664]{1,0:T(8,128)(2,1)} %unpack.6.refs_5_), channel_id=1, source_target_pairs={{0,4},{4,0},{8,12},{12,8},{16,20},{20,16},{24,28},{28,24},{1,5},{5... | collective-permute-start | bytes 2555912 | tf_op jit(solution)/shard_map/ppermute | solution.py:349
  258.3 28.8 %collective-permute-start.45 = (bf16[144,1664]{1,0:T(8,128)(2,1)}, bf16[144,1664]{1,0:T(8,128)(2,1)}, u32[]{:S(2)}, u32[]{:S(2)}) collective-permute-start(bf16[144,1664]{1,0:T(8,128)(2,1)} %get-tuple-element.154.refs_7_), channel_id=1, source_target_pairs={{0,24},{4,28},{8,0},{12,4},{16,8},{20,12},{24,16},{28,20},{1,25},{... | collective-permute-start | bytes 1437704 | tf_op jit(solution)/shard_map/ppermute | solution.py:346
  269.6 24.6 %collective-permute-start.53 = (bf16[256,1664]{1,0:T(8,128)(2,1)}, bf16[256,1664]{1,0:T(8,128)(2,1)}, u32[]{:S(2)}, u32[]{:S(2)}) collective-permute-start(bf16[256,1664]{1,0:T(8,128)(2,1)} %unpack.7.refs_5_), channel_id=1, source_target_pairs={{0,4},{4,0},{8,12},{12,8},{16,20},{20,16},{24,28},{28,24},{1,5},{5... | collective-permute-start | bytes 2555912 | tf_op jit(solution)/shard_map/ppermute | solution.py:349
  290.6 51.1 %collective-permute-start.50 = (bf16[144,1664]{1,0:T(8,128)(2,1)}, bf16[144,1664]{1,0:T(8,128)(2,1)S(1)}, u32[]{:S(2)}, u32[]{:S(2)}) collective-permute-start(bf16[144,1664]{1,0:T(8,128)(2,1)} %get-tuple-element.159), channel_id=1, source_target_pairs={{0,16},{4,20},{8,24},{12,28},{16,0},{20,4},{24,8},{28,12},{1,17},{... | collective-permute-start | bytes 1437704 | tf_op jit(solution)/shard_map/ppermute | solution.py:346
  290.7 53.9 %collective-permute-start.52 = (bf16[128,1664]{1,0:T(8,128)(2,1)}, bf16[128,1664]{1,0:T(8,128)(2,1)}, u32[]{:S(2)}, u32[]{:S(2)}) collective-permute-start(bf16[128,1664]{1,0:T(8,128)(2,1)} %get-tuple-element.158.refs_10_), channel_id=1, source_target_pairs={{0,24},{4,28},{8,0},{12,4},{16,8},{20,12},{24,16},{28,20},{1,25},{... | collective-permute-start | bytes 1277960 | tf_op jit(solution)/shard_map/ppermute | solution.py:346
  290.9 51.6 %collective-permute-start.51 = (bf16[144,1664]{1,0:T(8,128)(2,1)}, bf16[144,1664]{1,0:T(8,128)(2,1)}, u32[]{:S(2)}, u32[]{:S(2)}) collective-permute-start(bf16[144,1664]{1,0:T(8,128)(2,1)} %get-tuple-element.160.refs_7_), channel_id=1, source_target_pairs={{0,8},{4,12},{8,16},{12,20},{16,24},{20,28},{24,0},{28,4},{1,9},{5... | collective-permute-start | bytes 1437704 | tf_op jit(solution)/shard_map/ppermute | solution.py:346
  297.3 62.8 %collective-permute-start.54 = (bf16[128,1664]{1,0:T(8,128)(2,1)}, bf16[128,1664]{1,0:T(8,128)(2,1)}, u32[]{:S(2)}, u32[]{:S(2)}) collective-permute-start(bf16[128,1664]{1,0:T(8,128)(2,1)} %get-tuple-element.162), channel_id=1, source_target_pairs={{0,16},{4,20},{8,24},{12,28},{16,0},{20,4},{24,8},{28,12},{1,17},{... | collective-permute-start | bytes 1277960 | tf_op jit(solution)/shard_map/ppermute | solution.py:346
  300.1 59.9 %collective-permute-start.55 = (bf16[128,1664]{1,0:T(8,128)(2,1)}, bf16[128,1664]{1,0:T(8,128)(2,1)}, u32[]{:S(2)}, u32[]{:S(2)}) collective-permute-start(bf16[128,1664]{1,0:T(8,128)(2,1)} %get-tuple-element.163), channel_id=1, source_target_pairs={{0,8},{4,12},{8,16},{12,20},{16,24},{20,28},{24,0},{28,4},{1,9},{5... | collective-permute-start | bytes 1277960 | tf_op jit(solution)/shard_map/ppermute | solution.py:346
  (80 other events, 1207.1 us)
where the time goes:
time: 380 us; the launch traced here: 373 us
  waiting for transfers between devices  159 us (42%)
  Pallas kernels  89.6 us (24%)
  starting transfers between devices  69.2 us (18%)
  other arithmetic  28.2 us (7%)
  matrix products  14.6 us (4%)
  local copies, waits for them, and re-layouts  11 us (3%)
    ppermute x12, waiting for transfers between devices, along(): return lax.ppermute(value, 'expert', pairs)  80.9 us
    ppermute x36, waiting for transfers between devices, deal(): moved.append(lax.ppermute(blocks[d], 'segment', pairs))  75.4 us
    pallas_call x4, Pallas kernels, expert_unit(): pl.pallas_call(partial(expert_kernel, sections, images, split, len(after)...  47.3 us
    ppermute x36, starting transfers between devices, deal(): moved.append(lax.ppermute(blocks[d], 'segment', pairs))  27 us
    ppermute x12, starting transfers between devices, along(): return lax.ppermute(value, 'expert', pairs)  23.6 us
    pallas_call x6, Pallas kernels, unpack(): pl.pallas_call(partial(unpack_kernel, images, sections, len(addend), len(...  19.1 us
    pallas_call x6, Pallas kernels, pack(): pl.pallas_call(partial(pack_kernel, images, sections, inputs), name='pack...  17.4 us
    dot_general x2, matrix products, project_in(): jnp.dot(normed, in_projection, preferred_element_type=jnp.float32)  8.3 us
  transfers between devices with their start and end apart: 58, of which 23 were waited for; matrix products, arithmetic and copies ran while one was open for 10% of the time, Pallas kernels for 24%

commit v1 on v0

--- a/solution.py
+++ b/solution.py
@@ -77,35 +77,44 @@
     return jnp.concatenate(rows, axis=0)
 
 
-def pack_kernel(images, sections, inputs, *refs):
+def pack_kernel(images, sections, inputs, together, *refs):
     spots_ref, slots_ref = refs[:2]
     dense = refs[2 : 2 + inputs]
+    parts = 1 if together else sections
     if inputs > 1:
-        joined, blocks = refs[-1], refs[-1 - sections : -1]
+        joined, blocks = refs[-1], refs[-1 - parts : -1]
         seq_len = dense[0].shape[0]
         for i in range(images):
             joined[i * seq_len : (i + 1) * seq_len, :] = dense[i][...]
     else:
-        joined, blocks = dense[0], refs[-sections:]
-    count = blocks[0].shape[0]
+        joined, blocks = dense[0], refs[-parts:]
+    count = blocks[0].shape[-2]
     table = slot_table(spots_ref, slots_ref, images, sections, count).astype(jnp.bfloat16)
     total = jnp.dot(table, joined[...], preferred_element_type=jnp.float32).astype(jnp.bfloat16)
     for d in range(sections):
-        blocks[d][...] = total[d * count : (d + 1) * count, :]
-
-
-def pack(spots, slots, dense, capacity, after=()):
+        block = total[d * count : (d + 1) * count, :]
+        if together:
+            blocks[0][spots_ref[images + 1 + d]] = block
+        else:
+            blocks[d][...] = block
+
+
+def pack(spots, slots, dense, capacity, after=(), together=False):
     sections, seq_len = slots.shape[1:]
     width = dense[0].shape[1]
     inputs = len(dense)
     images = sum(block.shape[0] for block in dense) // seq_len
     count = images * capacity
     whole = pl.BlockSpec(memory_space=pltpu.VMEM)
-    shapes = [jax.ShapeDtypeStruct((count, width), jnp.bfloat16)] * sections
+    if together:
+        shapes = [jax.ShapeDtypeStruct((sections, count, width), jnp.bfloat16)]
+    else:
+        shapes = [jax.ShapeDtypeStruct((count, width), jnp.bfloat16)] * sections
+    parts = len(shapes)
     if inputs > 1:
         shapes.append(jax.ShapeDtypeStruct((images * seq_len, width), jnp.bfloat16))
     results = pl.pallas_call(
-        partial(pack_kernel, images, sections, inputs),
+        partial(pack_kernel, images, sections, inputs, together),
         name="pack",
         in_specs=[SCALARS] + [whole] * (1 + inputs) + [UNREAD] * len(after),
         out_specs=[whole] * len(shapes),
@@ -113,23 +122,24 @@
         compiler_params=params(),
         cost_estimate=SMALL,
     )(spots, slots, *dense, *after)
-    return results[:sections], results[sections:]
+    return results[:parts], results[parts:]
 
 
 EXTRA = 16
 
 
-def unpack_kernel(images, sections, extra, scored, *refs):
+def unpack_kernel(images, sections, parts, extra, scored, *refs):
     spots_ref, slots_ref = refs[:2]
-    blocks = refs[2 : 2 + sections]
-    addend = refs[2 + sections : 2 + sections + extra]
-    partners = refs[2 + sections + extra : 2 + sections + extra + scored]
+    blocks = refs[2 : 2 + parts]
+    addend = refs[2 + parts : 2 + parts + extra]
+    partners = refs[2 + parts + extra : 2 + parts + extra + scored]
     joined = refs[-1]
     dense = refs[-1 - (images if extra or scored else 1) : -1]
-    count = blocks[0].shape[0]
+    count = blocks[0].shape[-2]
     seq_len = slots_ref.shape[2]
     for d in range(sections):
-        joined[d * count : (d + 1) * count, :] = blocks[d][...]
+        block = blocks[d][...] if parts > 1 else blocks[0][spots_ref[images + 1 + d]]
+        joined[d * count : (d + 1) * count, :] = block
     table = slot_table(spots_ref, slots_ref, images, sections, count)
     total = jnp.dot(
         table.T.astype(jnp.bfloat16), joined[...], preferred_element_type=jnp.float32
@@ -137,7 +147,8 @@
     if scored:
         lines = []
         for d in range(sections):
-            product = blocks[d][...].astype(jnp.float32) * partners[d][...].astype(jnp.float32)
+            product = joined[d * count : (d + 1) * count, :].astype(jnp.float32)
+            product = product * partners[0][spots_ref[images + 1 + d]].astype(jnp.float32)
             column = jnp.sum(product, axis=1, keepdims=True)
             lines.append(
                 jnp.sum(table[d * count : (d + 1) * count, :] * column, axis=0, keepdims=True)
@@ -162,15 +173,15 @@
 
 def unpack(spots, slots, blocks, images, addend=(), partners=(), after=()):
     sections, seq_len = slots.shape[1:]
-    count, width = blocks[0].shape
+    count, width = blocks[0].shape[-2:]
     whole = pl.BlockSpec(memory_space=pltpu.VMEM)
-    inputs = sections + len(addend) + len(partners)
+    inputs = len(blocks) + len(addend) + len(partners)
     height = seq_len + (EXTRA if partners else 0)
     parts = images if addend or partners else 1
     if parts == 1:
         height = images * seq_len
     return pl.pallas_call(
-        partial(unpack_kernel, images, sections, len(addend), len(partners)),
+        partial(unpack_kernel, images, sections, len(blocks), len(addend), len(partners)),
         name="unpack",
         in_specs=[SCALARS] + [whole] * (1 + inputs) + [UNREAD] * len(after),
         out_specs=[whole] * parts,
@@ -181,39 +192,37 @@
     )(spots, slots, *blocks, *addend, *partners, *after)
 
 
-def merge_kernel(sections, *refs):
-    met = refs[sections]
-    merged = refs[-sections:]
-    count = merged[0].shape[0]
+def merge_kernel(sections, spots_ref, *refs):
+    met, merged = refs[sections], refs[-1]
+    count = merged.shape[1]
+    first = spots_ref.shape[0] - sections
     for d in range(sections):
         total = refs[d][...].astype(jnp.float32)
         total = total + met[d * count : (d + 1) * count, :].astype(jnp.float32)
-        merged[d][...] = total.astype(jnp.bfloat16)
-
-
-def merge(blocks, met, after=()):
+        merged[spots_ref[first + d]] = total.astype(jnp.bfloat16)
+
+
+def merge(spots, blocks, met, after=()):
     sections = len(blocks)
     whole = pl.BlockSpec(memory_space=pltpu.VMEM)
     return pl.pallas_call(
         partial(merge_kernel, sections),
         name="merge",
-        in_specs=[whole] * (sections + 1) + [UNREAD] * len(after),
-        out_specs=[whole] * sections,
-        out_shape=[jax.ShapeDtypeStruct(blocks[0].shape, jnp.bfloat16)] * sections,
+        in_specs=[SCALARS] + [whole] * (sections + 1) + [UNREAD] * len(after),
+        out_specs=whole,
+        out_shape=jax.ShapeDtypeStruct((sections,) + blocks[0].shape, jnp.bfloat16),
         compiler_params=params(),
         cost_estimate=SMALL,
-    )(*blocks, met, *after)
+    )(spots, *blocks, met, *after)
 
 
 def expert_kernel(sections, images, split, unread, *refs):
     spots_ref, other_ref, router_ref = refs[:3]
     mixed_in = refs[3 : 3 + sections]
-    pulls = 1 if split == 1 else sections
-    grads_in = refs[3 + sections : 3 + sections + pulls]
-    up_ref, down_ref = refs[3 + sections + pulls : 5 + sections + pulls]
-    outs = refs[5 + sections + pulls + unread :]
-    out_parts, grad_parts = outs[:split], outs[split : split + sections]
-    mixed, grads, out_sum, grad_sum, gate_ref = outs[split + sections :]
+    grads_in, up_ref, down_ref = refs[3 + sections : 6 + sections]
+    outs = refs[6 + sections + unread :]
+    mixed, grads, out_sum, grad_sum, gate_ref = outs[-5:]
+    out_parts, grad_parts = outs[:split], outs[split:-5]
     step, last = pl.program_id(0), pl.num_programs(0) - 1
     count = mixed_in[0].shape[0]
     total = count * sections
@@ -226,16 +235,13 @@
         others = []
         for d in range(sections):
             mixed[d * count : (d + 1) * count, :] = mixed_in[d][...]
-            if split > 1:
-                grads[d * count : (d + 1) * count, :] = grads_in[d][...]
+            grads[d * count : (d + 1) * count, :] = grads_in[spots_ref[images + 1 + d]]
             column = jnp.zeros((count, 1), jnp.int32)
             for i in range(images):
                 ids = other_ref[spots_ref[images + 1 + d], pl.ds(spots_ref[i], 1), :]
                 own = at_row == at_slot + i * capacity
                 column = column + jnp.sum(jnp.where(own, ids, 0), axis=1, keepdims=True)
             others.append(column)
-        if split == 1:
-            grads[...] = grads_in[0][...]
         logits = jnp.dot(mixed[...], router_ref[...], preferred_element_type=jnp.float32)
         lanes = lax.broadcasted_iota(jnp.int32, logits.shape, 1)
         mine = jnp.sum(jnp.where(lanes == spots_ref[images], logits, 0.0), axis=1, keepdims=True)
@@ -265,7 +271,11 @@
             rows = slice(part * size, (part + 1) * size)
             out_parts[part][...] = (out_sum[rows, :] * gate[rows, :]).astype(jnp.bfloat16)
         for d in range(sections):
-            grad_parts[d][...] = grad_sum[d * count : (d + 1) * count, :].astype(jnp.bfloat16)
+            block = grad_sum[d * count : (d + 1) * count, :].astype(jnp.bfloat16)
+            if split > 1:
+                grad_parts[0][spots_ref[images + 1 + d]] = block
+            else:
+                grad_parts[d][...] = block
 
 
 def expert_unit(spots, others, router, mixed_in, grads_in, up_local, down_local, split, after=()):
@@ -281,21 +291,22 @@
         return pl.BlockSpec(shape, lambda f: (0,) * len(shape))
 
     block = whole((count, width))
+    shapes = [(total // split, width)] * split
+    shapes += [(sections, count, width)] if split > 1 else [(count, width)] * sections
     results = pl.pallas_call(
         partial(expert_kernel, sections, images, split, len(after)),
         name="expert",
         grid=(hidden_units // tile,),
         in_specs=[SCALARS, whole(others.shape), whole(router.shape)]
         + [block] * sections
-        + [whole(block_in.shape) for block_in in grads_in]
+        + [whole(grads_in.shape)]
         + [
             pl.BlockSpec((width, tile), lambda f: (0, f)),
             pl.BlockSpec((tile, width), lambda f: (f, 0)),
         ]
         + [UNREAD] * len(after),
-        out_specs=[whole((total // split, width))] * split + [block] * sections,
-        out_shape=[jax.ShapeDtypeStruct((total // split, width), jnp.bfloat16)] * split
-        + [jax.ShapeDtypeStruct((count, width), jnp.bfloat16)] * sections,
+        out_specs=[whole(shape) for shape in shapes],
+        out_shape=[jax.ShapeDtypeStruct(shape, jnp.bfloat16) for shape in shapes],
         scratch_shapes=[
             pltpu.VMEM((total, width), jnp.bfloat16),
             pltpu.VMEM((total, width), jnp.bfloat16),
@@ -305,7 +316,7 @@
         ],
         compiler_params=params(),
         cost_estimate=SMALL,
-    )(spots, others, router, *mixed_in, *grads_in, up_local, down_local, *after)
+    )(spots, others, router, *mixed_in, grads_in, up_local, down_local, *after)
     return results[:split], results[split:]
 
 
@@ -355,13 +366,15 @@
             moved.append(lax.ppermute(blocks[d], "segment", pairs))
         return moved
 
+    def deal_whole(value):
+        return lax.all_to_all(value, "segment", split_axis=0, concat_axis=0, tiled=True)
+
     def deal_small(value):
         return lax.all_to_all(
             jnp.take(value, relative, axis=0), "segment", split_axis=0, concat_axis=0, tiled=True
         )
 
-    half = line // 2
-    chunks = [list(range(line - 1, half - 1, -1)), list(range(half - 1, -1, -1))]
+    chunks = [list(range(line - 2, -1, -2)), list(range(line - 1, 0, -2))]
 
     expert_list = jnp.arange(experts)
     hits = jnp.any(chosen.T[None] == expert_list[:, None, None], axis=1)
@@ -395,14 +408,18 @@
 
     spots = {(index, far): spots_of(index, far) for index in (0, 1) for far in (0, 1)}
 
-    cot_dense = {0: upstream, 1: along(upstream, 1)}
+    early = {1, line - 1}
+    cot_dense = {0: upstream}
+    for step in sorted(early):
+        cot_dense[step] = along(upstream, step)
     slots, late_upstream = lax.optimization_barrier((slots, upstream))
-    for step in range(2, line):
-        cot_dense[step] = along(late_upstream, step)
+    for step in range(1, line):
+        if step not in early:
+            cot_dense[step] = along(late_upstream, step)
 
     def cot_pack(index):
         dense = [cot_dense[step] for step in chunks[index]]
-        return pack(spots[index, 0], slots, dense, capacity)[0]
+        return pack(spots[index, 0], slots, dense, capacity, together=True)[0][0]
 
     joined, project_back = jax.vjp(
         partial(project_in, first_gain=first_gain, in_projection=in_projection), picture
@@ -410,11 +427,9 @@
     cot_packed, cot_rows = {}, {}
     cot_packed[1] = cot_pack(1)
     joined, cot_packed[1] = lax.optimization_barrier((joined, cot_packed[1]))
-    cot_rows[1, 0] = deal(cot_packed[1])
+    cot_rows[1, 0] = deal_whole(cot_packed[1])
     residual, attend_back = jax.vjp(partial(attend, out_projection=out_projection), picture, joined)
-    residual, cot_rows[1, 0], slot_others = lax.optimization_barrier(
-        (residual, cot_rows[1, 0], slot_others)
-    )
+    residual, slot_others = lax.optimization_barrier((residual, slot_others))
     normed, norm_back = jax.vjp(partial(layer_norm, gain_vector=second_gain), residual)
     mixed = normed.astype(jnp.bfloat16)
     own_logits = jnp.dot(mixed, router_weight, preferred_element_type=jnp.float32)
@@ -423,9 +438,9 @@
     for step in range(1, line):
         mixed_dense[step] = along(mixed, step)
 
-    cot_rows[1, 1] = [across(jnp.concatenate(cot_rows[1, 0], axis=0))]
+    cot_rows[1, 1] = across(cot_rows[1, 0])
     cot_packed[0] = cot_pack(0)
-    cot_rows[0, 0] = deal(cot_packed[0])
+    cot_rows[0, 0] = deal_whole(cot_packed[0])
 
     mixed_rows, far_dense = {}, {}
 
@@ -456,35 +471,40 @@
             after,
         )
         done = (grads[index, far][0],)
-        grads[index, far] = deal(grads[index, far])
+        if far:
+            grads[index, far] = deal(grads[index, far])
+        else:
+            grads[index, far] = [deal_whole(grads[index, far][0])]
         return done
 
-    done = mixed_pack(1, (cot_packed[0][0],))
-    done = mixed_pack(0, done + tuple(cot_rows[1, 1]))
-    cot_rows[0, 1] = [across(jnp.concatenate(cot_rows[0, 0], axis=0))]
+    done = mixed_pack(1, (cot_packed[0],))
+    done = mixed_pack(0, done + (cot_rows[1, 1],))
+    cot_rows[0, 1] = across(cot_rows[0, 0])
     done = far_pack(1, done)
-    done = unit(1, 0, done)
     done = far_pack(0, done)
-    done = unit(0, 0, done)
-    done = unit(1, 1, done + tuple(grads[1, 0][1:]))
+    done = unit(1, 0, done + tuple(mixed_rows[1, 1][1:]))
+    done = unit(0, 0, done + tuple(mixed_rows[0, 1][1:]))
+    done = unit(1, 1, done)
     met = {1: across(outs[1, 1][0])}
-    done = unit(0, 1, done + tuple(grads[0, 0][1:]))
+    done = unit(0, 1, done + tuple(grads[1, 0]))
     met[0] = across(outs[0, 1][0])
 
     grad_far, out_back, out_dense, grad_dense = {}, {}, {}, {}
     for index in (1, 0):
         count = len(chunks[index])
+        if index == 0:
+            done += tuple(grads[0, 0])
         grad_far[index] = unpack(spots[index, 1], slots, grads[index, 1], count, after=done)[0]
         done = (grad_far[index],)
         grad_far[index] = across(grad_far[index])
-        merged = merge(outs[index, 0], met[index], done)
-        done = (merged[0],)
-        out_back[index] = deal(merged)
+        merged = merge(spots[index, 0], outs[index, 0], met[index], done)
+        done = (merged,)
+        out_back[index] = deal_whole(merged)
     for index in (1, 0):
         chunk = chunks[index]
         count = len(chunk)
         out_block = unpack(
-            spots[index, 0], slots, out_back[index], count, (), cot_packed[index], done
+            spots[index, 0], slots, [out_back[index]], count, (), [cot_packed[index]], done
         )
         done = (out_block[0],)
         grad_block = unpack(

time: 380 us -> 426 us (1.12)
  waiting for transfers between devices: 159 us -> 210 us
  other arithmetic: 28.2 us -> 18.7 us
    all_to_all x0 -> x6, starting transfers between devices: none -> 26.9 us  [deal_whole(): lax.all_to_all(value, 'segment', split_axis=0, concat_axis=0, tiled=True)]
    ppermute x36 -> x18, waiting for transfers between devices: 75.4 us -> 99.3 us  [deal(): moved.append(lax.ppermute(blocks[d], 'segment', pairs))]
    ppermute x8, waiting for transfers between devices: 0.02 us -> 22.6 us  [across(): return lax.ppermute(value, 'expert', [(j, j ^ 1) for j in range(members)])]
    ppermute x36 -> x18, starting transfers between devices: 27 us -> 13 us  [deal(): moved.append(lax.ppermute(blocks[d], 'segment', pairs))]
    all_to_all x0 -> x6, waiting for transfers between devices: none -> 11.7 us  [deal_whole(): lax.all_to_all(value, 'segment', split_axis=0, concat_axis=0, tiled=True)]
    ppermute x12, waiting for transfers between devices: 80.9 us -> 71 us  [along(): return lax.ppermute(value, 'expert', pairs)]
    ppermute x12, starting transfers between devices: 23.6 us -> 17.1 us  [along(): return lax.ppermute(value, 'expert', pairs)]
    concatenate x2 -> x0, other arithmetic: 4.51 us -> none  [the longest x1 2.3 us: shards(): cot_rows[1, 1] = [across(jnp.concatenate(cot_rows[1, 0], axis=0))]]
  transfers between devices with their start and end apart: 58 -> 46, of which waited for: 23 -> 24; matrix products, arithmetic and copies ran while one was open for 10% -> 7% of each run, Pallas kernels for 24% -> 21%
where the time goes in v1:
time: 426 us; the launch traced here: 419 us
  waiting for transfers between devices  210 us (49%)
  Pallas kernels  89.8 us (21%)
  starting transfers between devices  72.8 us (17%)
  other arithmetic  18.7 us (4%)
  matrix products  15.3 us (4%)
  local copies, waits for them, and re-layouts  11.2 us (3%)
    ppermute x18, waiting for transfers between devices, deal(): moved.append(lax.ppermute(blocks[d], 'segment', pairs))  99.3 us
    ppermute x12, waiting for transfers between devices, along(): return lax.ppermute(value, 'expert', pairs)  71 us
    pallas_call x4, Pallas kernels, expert_unit(): pl.pallas_call(partial(expert_kernel, sections, images, split, len(after)...  47.3 us
    all_to_all x6, starting transfers between devices, deal_whole(): lax.all_to_all(value, 'segment', split_axis=0, concat_axis=0, tiled=True)  26.9 us
    ppermute x8, waiting for transfers between devices, across(): return lax.ppermute(value, 'expert', [(j, j ^ 1) for j in range(members)])  22.6 us
    pallas_call x6, Pallas kernels, unpack(): pl.pallas_call(partial(unpack_kernel, images, sections, len(blocks), len(...  19.2 us
    pallas_call x6, Pallas kernels, pack(): pl.pallas_call(partial(pack_kernel, images, sections, inputs, together),...  17.2 us
    ppermute x12, starting transfers between devices, along(): return lax.ppermute(value, 'expert', pairs)  17.1 us
  transfers between devices with their start and end apart: 46, of which 24 were waited for; matrix products, arithmetic and copies ran while one was open for 7% of the time, Pallas kernels for 21%

profile of v1, /device:TPU:0, one launch (start us, length us, event | category | flops | bytes accessed | tf_op | source)
XLA Modules:
  0.0 418.8 jit_solution(7082861909521765479)
XLA Ops:
  9.0 4.2 %all-to-all-start = ((s32[8,1,704]{2,1,0:T(1,128)}), s32[8,1,704]{2,1,0:T(1,128)S(1)}, u32[]{:S(2)}, u32[]{:S(2)}) async-start(s32[8,1,704]{2,1,0:T(1,128)} %all_to_all.27), calls=%async_computation | async-start | bytes 49152 | tf_op jit(solution)/shard_map/all_to_all | solution.py:396
  16.4 6.6 %convolution_convert_fusion = bf16[128,2496]{0,1:T(8,128)(2,1)} fusion(bf16[1664,2496]{0,1:T(8,128)(2,1)} %param.18, bf16[1,1,128,1664]{3,2,1,0:T(8,128)(2,1)S(1)} %copy-done.3, f32[1664]{0:T(1024)} %param.17, f32[128]{0:T(128)S(1)} %fusion.36, f32[128]{0:T(128)S(1)} %broadcast_multiply_fusion.1), kind=kOutput, calls=%fused_computation.3 | convolution fusion | flops 1064640512 | bytes 9379328 | tf_op jit(solution)/shard_map/jvp()/dot_general | solution.py:34
  40.4 4.3 %all-to-all-start.2 = ((bf16[4,96,1664]{2,1,0:T(8,128)(2,1)}), bf16[4,96,1664]{2,1,0:T(8,128)(2,1)}, u32[]{:S(2)}, u32[]{:S(2)}) async-start(bf16[4,96,1664]{2,1,0:T(8,128)(2,1)} %get-tuple-element.64.refs_3_), calls=%async_computation.2 | async-start | bytes 2555904 | tf_op jit(solution)/shard_map/all_to_all | solution.py:370
  50.1 11.7 %all-to-all-done.2.refs_7_ = bf16[4,96,1664]{2,1,0:T(8,128)(2,1)} async-done(((bf16[4,96,1664]{2,1,0:T(8,128)(2,1)}), bf16[4,96,1664]{2,1,0:T(8,128)(2,1)}, u32[]{:S(2)}, u32[]{:S(2)}) %all-to-all-start.2) | async-done | bytes 1277984 | tf_op jit(solution)/shard_map/all_to_all | solution.py:370
  71.4 7.4 %collective-permute-done.4.refs_3_ = bf16[128,1664]{1,0:T(8,128)(2,1)} collective-permute-done((bf16[128,1664]{1,0:T(8,128)(2,1)S(1)}, bf16[128,1664]{1,0:T(8,128)(2,1)}, u32[]{:S(2)}, u32[]{:S(2)}) %collective-permute-start.4) | collective-permute-done | bytes 426016 | tf_op jit(solution)/shard_map/ppermute | solution.py:357
  78.7 6.8 %collective-permute-done.3.refs_2_ = bf16[128,1664]{1,0:T(8,128)(2,1)} collective-permute-done((bf16[128,1664]{1,0:T(8,128)(2,1)S(1)}, bf16[128,1664]{1,0:T(8,128)(2,1)}, u32[]{:S(2)}, u32[]{:S(2)}) %collective-permute-start.3) | collective-permute-done | bytes 426016 | tf_op jit(solution)/shard_map/ppermute | solution.py:357
  90.1 12.9 %collective-permute-done.2.refs_2_ = bf16[128,1664]{1,0:T(8,128)(2,1)S(1)} collective-permute-done((bf16[128,1664]{1,0:T(8,128)(2,1)S(1)}, bf16[128,1664]{1,0:T(8,128)(2,1)S(1)}, u32[]{:S(2)}, u32[]{:S(2)}) %collective-permute-start.2) | collective-permute-done | bytes 426016 | tf_op jit(solution)/shard_map/ppermute | solution.py:357
  108.2 4.8 %all-to-all-start.3 = ((bf16[4,96,1664]{2,1,0:T(8,128)(2,1)}), bf16[4,96,1664]{2,1,0:T(8,128)(2,1)}, u32[]{:S(2)}, u32[]{:S(2)}) async-start(bf16[4,96,1664]{2,1,0:T(8,128)(2,1)} %get-tuple-element.62.refs_4_.refs_3_), calls=%async_computation.3 | async-start | bytes 2555904 | tf_op jit(solution)/shard_map/all_to_all | solution.py:370
  120.1 8.1 %collective-permute-done.13.refs_2_ = bf16[256,1664]{1,0:T(8,128)(2,1)} collective-permute-done((bf16[256,1664]{1,0:T(8,128)(2,1)}, bf16[256,1664]{1,0:T(8,128)(2,1)}, u32[]{:S(2)}, u32[]{:S(2)}) %collective-permute-start.13) | collective-permute-done | bytes 852000 | tf_op jit(solution)/shard_map/ppermute | solution.py:360
  131.9 5.4 %collective-permute-done.11.refs_5_ = bf16[96,1664]{1,0:T(8,128)(2,1)} collective-permute-done((bf16[96,1664]{1,0:T(8,128)(2,1)}, bf16[96,1664]{1,0:T(8,128)(2,1)}, u32[]{:S(2)}, u32[]{:S(2)}) %collective-permute-start.11) | collective-permute-done | bytes 319520 | tf_op jit(solution)/shard_map/ppermute | solution.py:366
  137.3 5.9 %collective-permute-done.12.refs_6_ = bf16[96,1664]{1,0:T(8,128)(2,1)} collective-permute-done((bf16[96,1664]{1,0:T(8,128)(2,1)}, bf16[96,1664]{1,0:T(8,128)(2,1)}, u32[]{:S(2)}, u32[]{:S(2)}) %collective-permute-start.12) | collective-permute-done | bytes 319520 | tf_op jit(solution)/shard_map/ppermute | solution.py:366
  143.8 7.2 %collective-permute-done.16.refs_12_.refs_5_ = bf16[96,1664]{1,0:T(8,128)(2,1)} collective-permute-done((bf16[96,1664]{1,0:T(8,128)(2,1)}, bf16[96,1664]{1,0:T(8,128)(2,1)}, u32[]{:S(2)}, u32[]{:S(2)}) %collective-permute-start.16) | collective-permute-done | bytes 319520 | tf_op jit(solution)/shard_map/ppermute | solution.py:366
  151.0 5.9 %collective-permute-done.17.refs_13_.refs_6_ = bf16[96,1664]{1,0:T(8,128)(2,1)} collective-permute-done((bf16[96,1664]{1,0:T(8,128)(2,1)}, bf16[96,1664]{1,0:T(8,128)(2,1)}, u32[]{:S(2)}, u32[]{:S(2)}) %collective-permute-start.17) | collective-permute-done | bytes 319520 | tf_op jit(solution)/shard_map/ppermute | solution.py:366
  156.9 11.9 %expert.4 = (bf16[96,1664]{1,0:T(8,128)(2,1)}, bf16[96,1664]{1,0:T(8,128)(2,1)}, bf16[96,1664]{1,0:T(8,128)(2,1)}, bf16[96,1664]{1,0:T(8,128)(2,1)}, bf16[4,96,1664]{2,1,0:T(8,128)(2,1)}) custom-call(s32[7]{0:T(128)} %add_add_fusion.4.refs_0_.spots_ref, s32[4,8,48]{2,1,0:T(8,128)} %reshape.209.refs_1_, bf16[1664,8]{1,0:T(8,128)(2,1)} %copy.59.refs_2_, ...), custom_call_target="tpu_custom_call" | custom-call | flops 1000 | bytes 1000 | tf_op jit(solution)/shard_map/expert/pallas_call | solution.py:296
  168.7 4.5 %all-to-all-start.4 = ((bf16[4,96,1664]{2,1,0:T(8,128)(2,1)}), bf16[4,96,1664]{2,1,0:T(8,128)(2,1)}, u32[]{:S(2)}, u32[]{:S(2)}) async-start(bf16[4,96,1664]{2,1,0:T(8,128)(2,1)} %get-tuple-element.79.refs_10_), calls=%async_computation.4 | async-start | bytes 2555904 | tf_op jit(solution)/shard_map/all_to_all | solution.py:370
  177.5 19.0 %collective-permute-done.9.refs_6_ = bf16[96,1664]{1,0:T(8,128)(2,1)S(1)} collective-permute-done((bf16[96,1664]{1,0:T(8,128)(2,1)}, bf16[96,1664]{1,0:T(8,128)(2,1)S(1)}, u32[]{:S(2)}, u32[]{:S(2)}) %collective-permute-start.9) | collective-permute-done | bytes 319520 | tf_op jit(solution)/shard_map/ppermute | solution.py:366
  196.5 7.8 %collective-permute-done.19.refs_12_.refs_5_ = bf16[96,1664]{1,0:T(8,128)(2,1)S(1)} collective-permute-done((bf16[96,1664]{1,0:T(8,128)(2,1)}, bf16[96,1664]{1,0:T(8,128)(2,1)S(1)}, u32[]{:S(2)}, u32[]{:S(2)}) %collective-permute-start.19) | collective-permute-done | bytes 319520 | tf_op jit(solution)/shard_map/ppermute | solution.py:366
  204.3 6.0 %collective-permute-done.20.refs_13_.refs_6_ = bf16[96,1664]{1,0:T(8,128)(2,1)} collective-permute-done((bf16[96,1664]{1,0:T(8,128)(2,1)}, bf16[96,1664]{1,0:T(8,128)(2,1)}, u32[]{:S(2)}, u32[]{:S(2)}) %collective-permute-start.20) | collective-permute-done | bytes 319520 | tf_op jit(solution)/shard_map/ppermute | solution.py:366
  210.3 11.9 %expert.5 = (bf16[96,1664]{1,0:T(8,128)(2,1)}, bf16[96,1664]{1,0:T(8,128)(2,1)}, bf16[96,1664]{1,0:T(8,128)(2,1)}, bf16[96,1664]{1,0:T(8,128)(2,1)}, bf16[4,96,1664]{2,1,0:T(8,128)(2,1)}) custom-call(s32[7]{0:T(128)} %get-tuple-element.126.refs_0_.spots_ref, s32[4,8,48]{2,1,0:T(8,128)} %reshape.209.refs_1_, bf16[1664,8]{1,0:T(8,128)(2,1)} %copy.59.refs_2_, ...), custom_call_target="tpu_custom_call" | custom-call | flops 1000 | bytes 1000 | tf_op jit(solution)/shard_map/expert/pallas_call | solution.py:296
  222.2 11.7 %expert.6 = (bf16[384,1664]{1,0:T(8,128)(2,1)}, bf16[96,1664]{1,0:T(8,128)(2,1)}, bf16[96,1664]{1,0:T(8,128)(2,1)}, bf16[96,1664]{1,0:T(8,128)(2,1)}, bf16[96,1664]{1,0:T(8,128)(2,1)}) custom-call(s32[7]{0:T(128)} %get-tuple-element.124.refs_0_, s32[4,8,48]{2,1,0:T(8,128)} %reshape.209.refs_1_, bf16[1664,8]{1,0:T(8,128)(2,1)} %copy.59.refs_2_, ...), custom_call_target="tpu_custom_call" | custom-call | flops 1000 | bytes 1000 | tf_op jit(solution)/shard_map/expert/pallas_call | solution.py:296
  234.5 4.5 %all-to-all-start.5 = ((bf16[4,96,1664]{2,1,0:T(8,128)(2,1)}), bf16[4,96,1664]{2,1,0:T(8,128)(2,1)}, u32[]{:S(2)}, u32[]{:S(2)}) async-start(bf16[4,96,1664]{2,1,0:T(8,128)(2,1)} %get-tuple-element.87.refs_10_), calls=%async_computation.5 | async-start | bytes 2555904 | tf_op jit(solution)/shard_map/all_to_all | solution.py:370
  241.2 11.8 %expert.7 = (bf16[384,1664]{1,0:T(8,128)(2,1)}, bf16[96,1664]{1,0:T(8,128)(2,1)}, bf16[96,1664]{1,0:T(8,128)(2,1)}, bf16[96,1664]{1,0:T(8,128)(2,1)}, bf16[96,1664]{1,0:T(8,128)(2,1)}) custom-call(s32[7]{0:T(128)} %get-tuple-element.125.refs_0_, s32[4,8,48]{2,1,0:T(8,128)} %reshape.209.refs_1_, bf16[1664,8]{1,0:T(8,128)(2,1)} %copy.59.refs_2_, ...), custom_call_target="tpu_custom_call" | custom-call | flops 1000 | bytes 1000 | tf_op jit(solution)/shard_map/expert/pallas_call | solution.py:296
  254.4 8.7 %collective-permute-done.28.refs_4_ = bf16[96,1664]{1,0:T(8,128)(2,1)S(1)} collective-permute-done((bf16[96,1664]{1,0:T(8,128)(2,1)}, bf16[96,1664]{1,0:T(8,128)(2,1)S(1)}, u32[]{:S(2)}, u32[]{:S(2)}) %collective-permute-start.28) | collective-permute-done | bytes 319520 | tf_op jit(solution)/shard_map/ppermute | solution.py:366
  263.2 6.0 %collective-permute-done.29.refs_5_ = bf16[96,1664]{1,0:T(8,128)(2,1)} collective-permute-done((bf16[96,1664]{1,0:T(8,128)(2,1)}, bf16[96,1664]{1,0:T(8,128)(2,1)}, u32[]{:S(2)}, u32[]{:S(2)}) %collective-permute-start.29) | collective-permute-done | bytes 319520 | tf_op jit(solution)/shard_map/ppermute | solution.py:366
  275.1 4.3 %all-to-all-start.7 = ((bf16[4,96,1664]{2,1,0:T(8,128)(2,1)}), bf16[4,96,1664]{2,1,0:T(8,128)(2,1)}, u32[]{:S(2)}, u32[]{:S(2)}) async-start(bf16[4,96,1664]{2,1,0:T(8,128)(2,1)} %merge.2.refs_6_), calls=%async_computation.7 | async-start | bytes 2555904 | tf_op jit(solution)/shard_map/all_to_all | solution.py:370
  282.2 21.5 %collective-permute-done.24.refs_4_ = bf16[96,1664]{1,0:T(8,128)(2,1)} collective-permute-done((bf16[96,1664]{1,0:T(8,128)(2,1)}, bf16[96,1664]{1,0:T(8,128)(2,1)}, u32[]{:S(2)}, u32[]{:S(2)}) %collective-permute-start.24) | collective-permute-done | bytes 319520 | tf_op jit(solution)/shard_map/ppermute | solution.py:366
  303.7 5.9 %collective-permute-done.25.refs_5_ = bf16[96,1664]{1,0:T(8,128)(2,1)} collective-permute-done((bf16[96,1664]{1,0:T(8,128)(2,1)}, bf16[96,1664]{1,0:T(8,128)(2,1)}, u32[]{:S(2)}, u32[]{:S(2)}) %collective-permute-start.25) | collective-permute-done | bytes 319520 | tf_op jit(solution)/shard_map/ppermute | solution.py:366
  315.6 4.5 %all-to-all-start.6 = ((bf16[4,96,1664]{2,1,0:T(8,128)(2,1)}), bf16[4,96,1664]{2,1,0:T(8,128)(2,1)}, u32[]{:S(2)}, u32[]{:S(2)}) async-start(bf16[4,96,1664]{2,1,0:T(8,128)(2,1)} %merge.3.refs_4_), calls=%async_computation.6 | async-start | bytes 2555904 | tf_op jit(solution)/shard_map/all_to_all | solution.py:370
  329.2 13.1 %collective-permute-done.30.refs_3_ = bf16[256,1664]{1,0:T(8,128)(2,1)} collective-permute-done((bf16[256,1664]{1,0:T(8,128)(2,1)}, bf16[256,1664]{1,0:T(8,128)(2,1)}, u32[]{:S(2)}, u32[]{:S(2)}) %collective-permute-start.30) | collective-permute-done | bytes 852000 | tf_op jit(solution)/shard_map/ppermute | solution.py:360
  350.8 3.5 unpack.10
  363.8 33.9 %collective-permute-done.33 = bf16[144,1664]{1,0:T(8,128)(2,1)S(1)} collective-permute-done((bf16[144,1664]{1,0:T(8,128)(2,1)}, bf16[144,1664]{1,0:T(8,128)(2,1)S(1)}, u32[]{:S(2)}, u32[]{:S(2)}) %collective-permute-start.33) | collective-permute-done | bytes 479264 | tf_op jit(solution)/shard_map/ppermute | solution.py:357
  400.0 6.9 %collective-permute-done.36 = bf16[128,1664]{1,0:T(8,128)(2,1)} collective-permute-done((bf16[128,1664]{1,0:T(8,128)(2,1)}, bf16[128,1664]{1,0:T(8,128)(2,1)}, u32[]{:S(2)}, u32[]{:S(2)}) %collective-permute-start.36) | collective-permute-done | bytes 426016 | tf_op jit(solution)/shard_map/ppermute | solution.py:357
  (251 shorter events, 128.8 us)
Async XLA Ops:
  0.7 36.1 %collective-permute-start.1 = (bf16[128,1664]{1,0:T(8,128)(2,1)}, bf16[128,1664]{1,0:T(8,128)(2,1)}, u32[]{:S(2)}, u32[]{:S(2)}) collective-permute-start(bf16[128,1664]{1,0:T(8,128)(2,1)} %bitcast.99), channel_id=1, source_target_pairs={{0,8},{4,12},{8,16},{12,20},{16,24},{20,28},{24,0},{28,4},{1,9},{5... | collective-permute-start | bytes 1277960 | tf_op jit(solution)/shard_map/ppermute | solution.py:357
  3.7 33.0 %collective-permute-start = (bf16[128,1664]{1,0:T(8,128)(2,1)}, bf16[128,1664]{1,0:T(8,128)(2,1)}, u32[]{:S(2)}, u32[]{:S(2)}) collective-permute-start(bf16[128,1664]{1,0:T(8,128)(2,1)} %bitcast.100), channel_id=1, source_target_pairs={{0,24},{4,28},{8,0},{12,4},{16,8},{20,12},{24,16},{28,20},{1,25},{... | collective-permute-start | bytes 1277960 | tf_op jit(solution)/shard_map/ppermute | solution.py:357
  32.3 36.2 %collective-permute-start.5 = (bf16[128,1664]{1,0:T(8,128)(2,1)}, bf16[128,1664]{1,0:T(8,128)(2,1)}, u32[]{:S(2)}, u32[]{:S(2)}) collective-permute-start(bf16[128,1664]{1,0:T(8,128)(2,1)} %bitcast.101), channel_id=1, source_target_pairs={{0,16},{4,20},{8,24},{12,28},{16,0},{20,4},{24,8},{28,12},{1,17},{... | collective-permute-start | bytes 1277960 | tf_op jit(solution)/shard_map/ppermute | solution.py:357
  61.7 41.2 %collective-permute-start.6 = (bf16[4,96,1664]{2,1,0:T(8,128)(2,1)}, bf16[4,96,1664]{2,1,0:T(8,128)(2,1)}, u32[]{:S(2)}, u32[]{:S(2)}) collective-permute-start(bf16[4,96,1664]{2,1,0:T(8,128)(2,1)} %all-to-all-done.2.refs_7_), channel_id=1, source_target_pairs={{0,4},{4,0},{8,12},{12,8},{16,20},{20,16},{24,28},{28,24},{1,5},{5... | collective-permute-start | bytes 3833864 | tf_op jit(solution)/shard_map/ppermute | solution.py:360
  67.9 35.1 %collective-permute-start.2 = (bf16[128,1664]{1,0:T(8,128)(2,1)S(1)}, bf16[128,1664]{1,0:T(8,128)(2,1)S(1)}, u32[]{:S(2)}, u32[]{:S(2)}) collective-permute-start(bf16[128,1664]{1,0:T(8,128)(2,1)S(1)} %multiply_convert_fusion.refs_3_), channel_id=1, source_target_pairs={{0,16},{4,20},{8,24},{12,28},{16,0},{20,4},{24,8},{28,12},{1,17},{... | collective-permute-start | bytes 1277960 | tf_op jit(solution)/shard_map/ppermute | solution.py:357
  88.6 26.7 %collective-permute-start.14 = (bf16[256,1664]{1,0:T(8,128)(2,1)}, bf16[256,1664]{1,0:T(8,128)(2,1)}, u32[]{:S(2)}, u32[]{:S(2)}) collective-permute-start(bf16[256,1664]{1,0:T(8,128)(2,1)} %get-tuple-element.73), channel_id=1, source_target_pairs={{0,4},{4,0},{8,12},{12,8},{16,20},{20,16},{24,28},{28,24},{1,5},{5... | collective-permute-start | bytes 2555912 | tf_op jit(solution)/shard_map/ppermute | solution.py:360
  108.2 60.6 %all-to-all-start.3 = ((bf16[4,96,1664]{2,1,0:T(8,128)(2,1)}), bf16[4,96,1664]{2,1,0:T(8,128)(2,1)}, u32[]{:S(2)}, u32[]{:S(2)}) async-start(bf16[4,96,1664]{2,1,0:T(8,128)(2,1)} %get-tuple-element.62.refs_4_.refs_3_), calls=%async_computation.3 | async-start | bytes 2555904 | tf_op jit(solution)/shard_map/all_to_all | solution.py:370
  113.5 23.8 %collective-permute-start.11 = (bf16[96,1664]{1,0:T(8,128)(2,1)}, bf16[96,1664]{1,0:T(8,128)(2,1)}, u32[]{:S(2)}, u32[]{:S(2)}) collective-permute-start(bf16[96,1664]{1,0:T(8,128)(2,1)} %get-tuple-element.70), channel_id=1, source_target_pairs={{0,2},{1,3},{2,0},{3,1},{4,6},{5,7},{6,4},{7,5},{8,10},{9,11},{10,... | collective-permute-start | bytes 958472 | tf_op jit(solution)/shard_map/ppermute | solution.py:366
  115.2 27.9 %collective-permute-start.12 = (bf16[96,1664]{1,0:T(8,128)(2,1)}, bf16[96,1664]{1,0:T(8,128)(2,1)}, u32[]{:S(2)}, u32[]{:S(2)}) collective-permute-start(bf16[96,1664]{1,0:T(8,128)(2,1)} %get-tuple-element.71), channel_id=1, source_target_pairs={{0,3},{1,2},{2,1},{3,0},{4,7},{5,6},{6,5},{7,4},{8,11},{9,10},{10,... | collective-permute-start | bytes 958472 | tf_op jit(solution)/shard_map/ppermute | solution.py:366
  117.9 25.9 %collective-permute-start.15 = (bf16[96,1664]{1,0:T(8,128)(2,1)}, bf16[96,1664]{1,0:T(8,128)(2,1)S(1)}, u32[]{:S(2)}, u32[]{:S(2)}) collective-permute-start(bf16[96,1664]{1,0:T(8,128)(2,1)} %get-tuple-element.76), channel_id=1, source_target_pairs={{0,1},{1,0},{2,3},{3,2},{4,5},{5,4},{6,7},{7,6},{8,9},{9,8},{10,11... | collective-permute-start | bytes 958472 | tf_op jit(solution)/shard_map/ppermute | solution.py:366
  118.4 32.6 %collective-permute-start.16 = (bf16[96,1664]{1,0:T(8,128)(2,1)}, bf16[96,1664]{1,0:T(8,128)(2,1)}, u32[]{:S(2)}, u32[]{:S(2)}) collective-permute-start(bf16[96,1664]{1,0:T(8,128)(2,1)} %get-tuple-element.77), channel_id=1, source_target_pairs={{0,2},{1,3},{2,0},{3,1},{4,6},{5,7},{6,4},{7,5},{8,10},{9,11},{10,... | collective-permute-start | bytes 958472 | tf_op jit(solution)/shard_map/ppermute | solution.py:366
  128.2 28.7 %collective-permute-start.17 = (bf16[96,1664]{1,0:T(8,128)(2,1)}, bf16[96,1664]{1,0:T(8,128)(2,1)}, u32[]{:S(2)}, u32[]{:S(2)}) collective-permute-start(bf16[96,1664]{1,0:T(8,128)(2,1)} %get-tuple-element.78), channel_id=1, source_target_pairs={{0,3},{1,2},{2,1},{3,0},{4,7},{5,6},{6,5},{7,4},{8,11},{9,10},{10,... | collective-permute-start | bytes 958472 | tf_op jit(solution)/shard_map/ppermute | solution.py:366
  137.3 38.4 %collective-permute-start.7 = (bf16[96,1664]{1,0:T(8,128)(2,1)}, bf16[96,1664]{1,0:T(8,128)(2,1)}, u32[]{:S(2)}, u32[]{:S(2)}) collective-permute-start(bf16[96,1664]{1,0:T(8,128)(2,1)} %get-tuple-element.66), channel_id=1, source_target_pairs={{0,1},{1,0},{2,3},{3,2},{4,5},{5,4},{6,7},{7,6},{8,9},{9,8},{10,11... | collective-permute-start | bytes 958472 | tf_op jit(solution)/shard_map/ppermute | solution.py:366
  143.2 33.7 %collective-permute-start.8 = (bf16[96,1664]{1,0:T(8,128)(2,1)}, bf16[96,1664]{1,0:T(8,128)(2,1)}, u32[]{:S(2)}, u32[]{:S(2)}) collective-permute-start(bf16[96,1664]{1,0:T(8,128)(2,1)} %get-tuple-element.67), channel_id=1, source_target_pairs={{0,2},{1,3},{2,0},{3,1},{4,6},{5,7},{6,4},{7,5},{8,10},{9,11},{10,... | collective-permute-start | bytes 958472 | tf_op jit(solution)/shard_map/ppermute | solution.py:366
  168.7 65.7 %all-to-all-start.4 = ((bf16[4,96,1664]{2,1,0:T(8,128)(2,1)}), bf16[4,96,1664]{2,1,0:T(8,128)(2,1)}, u32[]{:S(2)}, u32[]{:S(2)}) async-start(bf16[4,96,1664]{2,1,0:T(8,128)(2,1)} %get-tuple-element.79.refs_10_), calls=%async_computation.4 | async-start | bytes 2555904 | tf_op jit(solution)/shard_map/all_to_all | solution.py:370
  175.4 28.9 %collective-permute-start.19 = (bf16[96,1664]{1,0:T(8,128)(2,1)}, bf16[96,1664]{1,0:T(8,128)(2,1)S(1)}, u32[]{:S(2)}, u32[]{:S(2)}) collective-permute-start(bf16[96,1664]{1,0:T(8,128)(2,1)} %get-tuple-element.81), channel_id=1, source_target_pairs={{0,2},{1,3},{2,0},{3,1},{4,6},{5,7},{6,4},{7,5},{8,10},{9,11},{10,... | collective-permute-start | bytes 958472 | tf_op jit(solution)/shard_map/ppermute | solution.py:366
  175.7 34.6 %collective-permute-start.20 = (bf16[96,1664]{1,0:T(8,128)(2,1)}, bf16[96,1664]{1,0:T(8,128)(2,1)}, u32[]{:S(2)}, u32[]{:S(2)}) collective-permute-start(bf16[96,1664]{1,0:T(8,128)(2,1)} %get-tuple-element.82), channel_id=1, source_target_pairs={{0,3},{1,2},{2,1},{3,0},{4,7},{5,6},{6,5},{7,4},{8,11},{9,10},{10,... | collective-permute-start | bytes 958472 | tf_op jit(solution)/shard_map/ppermute | solution.py:366
  176.9 64.3 %collective-permute-start.21 = (bf16[4,96,1664]{2,1,0:T(8,128)(2,1)}, bf16[4,96,1664]{2,1,0:T(8,128)(2,1)}, u32[]{:S(2)}, u32[]{:S(2)}) collective-permute-start(bf16[4,96,1664]{2,1,0:T(8,128)(2,1)} %all-to-all-done.3.refs_7_), channel_id=1, source_target_pairs={{0,4},{4,0},{8,12},{12,8},{16,20},{20,16},{24,28},{28,24},{1,5},{5... | collective-permute-start | bytes 3833864 | tf_op jit(solution)/shard_map/ppermute | solution.py:360
  233.9 38.2 %collective-permute-start.26 = (bf16[384,1664]{1,0:T(8,128)(2,1)}, bf16[384,1664]{1,0:T(8,128)(2,1)}, u32[]{:S(2)}, u32[]{:S(2)}) collective-permute-start(bf16[384,1664]{1,0:T(8,128)(2,1)} %get-tuple-element.98), channel_id=1, source_target_pairs={{0,4},{4,0},{8,12},{12,8},{16,20},{20,16},{24,28},{28,24},{1,5},{5... | collective-permute-start | bytes 3833864 | tf_op jit(solution)/shard_map/ppermute | solution.py:360
  234.5 40.7 %all-to-all-start.5 = ((bf16[4,96,1664]{2,1,0:T(8,128)(2,1)}), bf16[4,96,1664]{2,1,0:T(8,128)(2,1)}, u32[]{:S(2)}, u32[]{:S(2)}) async-start(bf16[4,96,1664]{2,1,0:T(8,128)(2,1)} %get-tuple-element.87.refs_10_), calls=%async_computation.5 | async-start | bytes 2555904 | tf_op jit(solution)/shard_map/all_to_all | solution.py:370
  239.5 23.7 %collective-permute-start.28 = (bf16[96,1664]{1,0:T(8,128)(2,1)}, bf16[96,1664]{1,0:T(8,128)(2,1)S(1)}, u32[]{:S(2)}, u32[]{:S(2)}) collective-permute-start(bf16[96,1664]{1,0:T(8,128)(2,1)} %get-tuple-element.100), channel_id=1, source_target_pairs={{0,2},{1,3},{2,0},{3,1},{4,6},{5,7},{6,4},{7,5},{8,10},{9,11},{10,... | collective-permute-start | bytes 958472 | tf_op jit(solution)/shard_map/ppermute | solution.py:366
  241.2 27.9 %collective-permute-start.29 = (bf16[96,1664]{1,0:T(8,128)(2,1)}, bf16[96,1664]{1,0:T(8,128)(2,1)}, u32[]{:S(2)}, u32[]{:S(2)}) collective-permute-start(bf16[96,1664]{1,0:T(8,128)(2,1)} %get-tuple-element.101), channel_id=1, source_target_pairs={{0,3},{1,2},{2,1},{3,0},{4,7},{5,6},{6,5},{7,4},{8,11},{9,10},{10,... | collective-permute-start | bytes 958472 | tf_op jit(solution)/shard_map/ppermute | solution.py:366
  253.0 59.5 %collective-permute-start.22 = (bf16[384,1664]{1,0:T(8,128)(2,1)}, bf16[384,1664]{1,0:T(8,128)(2,1)}, u32[]{:S(2)}, u32[]{:S(2)}) collective-permute-start(bf16[384,1664]{1,0:T(8,128)(2,1)} %get-tuple-element.89), channel_id=1, source_target_pairs={{0,4},{4,0},{8,12},{12,8},{16,20},{20,16},{24,28},{28,24},{1,5},{5... | collective-permute-start | bytes 3833864 | tf_op jit(solution)/shard_map/ppermute | solution.py:360
  275.1 40.5 %all-to-all-start.7 = ((bf16[4,96,1664]{2,1,0:T(8,128)(2,1)}), bf16[4,96,1664]{2,1,0:T(8,128)(2,1)}, u32[]{:S(2)}, u32[]{:S(2)}) async-start(bf16[4,96,1664]{2,1,0:T(8,128)(2,1)} %merge.2.refs_6_), calls=%async_computation.7 | async-start | bytes 2555904 | tf_op jit(solution)/shard_map/all_to_all | solution.py:370
  280.1 23.6 %collective-permute-start.24 = (bf16[96,1664]{1,0:T(8,128)(2,1)}, bf16[96,1664]{1,0:T(8,128)(2,1)}, u32[]{:S(2)}, u32[]{:S(2)}) collective-permute-start(bf16[96,1664]{1,0:T(8,128)(2,1)} %get-tuple-element.92), channel_id=1, source_target_pairs={{0,2},{1,3},{2,0},{3,1},{4,6},{5,7},{6,4},{7,5},{8,10},{9,11},{10,... | collective-permute-start | bytes 958472 | tf_op jit(solution)/shard_map/ppermute | solution.py:366
  281.6 28.1 %collective-permute-start.25 = (bf16[96,1664]{1,0:T(8,128)(2,1)}, bf16[96,1664]{1,0:T(8,128)(2,1)}, u32[]{:S(2)}, u32[]{:S(2)}) collective-permute-start(bf16[96,1664]{1,0:T(8,128)(2,1)} %get-tuple-element.93), channel_id=1, source_target_pairs={{0,3},{1,2},{2,1},{3,0},{4,7},{5,6},{6,5},{7,4},{8,11},{9,10},{10,... | collective-permute-start | bytes 958472 | tf_op jit(solution)/shard_map/ppermute | solution.py:366
  315.6 35.1 %all-to-all-start.6 = ((bf16[4,96,1664]{2,1,0:T(8,128)(2,1)}), bf16[4,96,1664]{2,1,0:T(8,128)(2,1)}, u32[]{:S(2)}, u32[]{:S(2)}) async-start(bf16[4,96,1664]{2,1,0:T(8,128)(2,1)} %merge.3.refs_4_), calls=%async_computation.6 | async-start | bytes 2555904 | tf_op jit(solution)/shard_map/all_to_all | solution.py:370
  322.9 37.0 %collective-permute-start.34 = (bf16[256,1664]{1,0:T(8,128)(2,1)}, bf16[256,1664]{1,0:T(8,128)(2,1)}, u32[]{:S(2)}, u32[]{:S(2)}) collective-permute-start(bf16[256,1664]{1,0:T(8,128)(2,1)} %unpack.7.refs_5_), channel_id=1, source_target_pairs={{0,4},{4,0},{8,12},{12,8},{16,20},{20,16},{24,28},{28,24},{1,5},{5... | collective-permute-start | bytes 2555912 | tf_op jit(solution)/shard_map/ppermute | solution.py:360
  345.4 54.6 %collective-permute-start.35 = (bf16[128,1664]{1,0:T(8,128)(2,1)}, bf16[128,1664]{1,0:T(8,128)(2,1)}, u32[]{:S(2)}, u32[]{:S(2)}) collective-permute-start(bf16[128,1664]{1,0:T(8,128)(2,1)} %get-tuple-element.108), channel_id=1, source_target_pairs={{0,24},{4,28},{8,0},{12,4},{16,8},{20,12},{24,16},{28,20},{1,25},{... | collective-permute-start | bytes 1277960 | tf_op jit(solution)/shard_map/ppermute | solution.py:357
  346.6 53.4 %collective-permute-start.37 = (bf16[128,1664]{1,0:T(8,128)(2,1)}, bf16[128,1664]{1,0:T(8,128)(2,1)}, u32[]{:S(2)}, u32[]{:S(2)}) collective-permute-start(bf16[128,1664]{1,0:T(8,128)(2,1)} %get-tuple-element.103.refs_4_), channel_id=1, source_target_pairs={{0,8},{4,12},{8,16},{12,20},{16,24},{20,28},{24,0},{28,4},{1,9},{5... | collective-permute-start | bytes 1277960 | tf_op jit(solution)/shard_map/ppermute | solution.py:357
  354.3 43.4 %collective-permute-start.33 = (bf16[144,1664]{1,0:T(8,128)(2,1)}, bf16[144,1664]{1,0:T(8,128)(2,1)S(1)}, u32[]{:S(2)}, u32[]{:S(2)}) collective-permute-start(bf16[144,1664]{1,0:T(8,128)(2,1)} %get-tuple-element.106.refs_4_), channel_id=1, source_target_pairs={{0,16},{4,20},{8,24},{12,28},{16,0},{20,4},{24,8},{28,12},{1,17},{... | collective-permute-start | bytes 1437704 | tf_op jit(solution)/shard_map/ppermute | solution.py:357
  363.1 43.8 %collective-permute-start.36 = (bf16[128,1664]{1,0:T(8,128)(2,1)}, bf16[128,1664]{1,0:T(8,128)(2,1)}, u32[]{:S(2)}, u32[]{:S(2)}) collective-permute-start(bf16[128,1664]{1,0:T(8,128)(2,1)} %get-tuple-element.109), channel_id=1, source_target_pairs={{0,16},{4,20},{8,24},{12,28},{16,0},{20,4},{24,8},{28,12},{1,17},{... | collective-permute-start | bytes 1277960 | tf_op jit(solution)/shard_map/ppermute | solution.py:357
  (61 other events, 783.1 us)

commit v2 on v1

--- a/solution.py
+++ b/solution.py
@@ -374,7 +374,8 @@
             jnp.take(value, relative, axis=0), "segment", split_axis=0, concat_axis=0, tiled=True
         )
 
-    chunks = [list(range(line - 2, -1, -2)), list(range(line - 1, 0, -2))]
+    half = line // 2
+    chunks = [list(range(line - 1, half - 1, -1)), list(range(half - 1, -1, -1))]
 
     expert_list = jnp.arange(experts)
     hits = jnp.any(chosen.T[None] == expert_list[:, None, None], axis=1)
@@ -408,7 +409,7 @@
 
     spots = {(index, far): spots_of(index, far) for index in (0, 1) for far in (0, 1)}
 
-    early = {1, line - 1}
+    early = {1}
     cot_dense = {0: upstream}
     for step in sorted(early):
         cot_dense[step] = along(upstream, step)
@@ -447,7 +448,7 @@
     def mixed_pack(index, after):
         dense = [mixed_dense[step] for step in chunks[index]]
         blocks, joined_dense = pack(spots[index, 0], slots, dense, capacity, after)
-        far_dense[index] = across(joined_dense[0])
+        far_dense[index] = joined_dense[0]
         mixed_rows[index, 0] = deal(blocks)
         return (blocks[0],)
 
@@ -477,45 +478,61 @@
             grads[index, far] = [deal_whole(grads[index, far][0])]
         return done
 
-    done = mixed_pack(1, (cot_packed[0],))
-    done = mixed_pack(0, done + (cot_rows[1, 1],))
+    done = mixed_pack(0, (cot_rows[1, 1], cot_rows[0, 0], mixed_dense[1]))
+    far_dense[0] = across(far_dense[0])
+    done = mixed_pack(1, done)
     cot_rows[0, 1] = across(cot_rows[0, 0])
+    done = far_pack(0, done)
+    done = unit(0, 0, done)
+    far_dense[1], cot_rows[0, 1] = lax.optimization_barrier((far_dense[1], cot_rows[0, 1]))
+    far_dense[1] = across(far_dense[1])
+    done = unit(0, 1, done)
+    met = {0: across(outs[0, 1][0])}
+    done = unit(1, 0, done)
     done = far_pack(1, done)
-    done = far_pack(0, done)
-    done = unit(1, 0, done + tuple(mixed_rows[1, 1][1:]))
-    done = unit(0, 0, done + tuple(mixed_rows[0, 1][1:]))
-    done = unit(1, 1, done)
-    met = {1: across(outs[1, 1][0])}
-    done = unit(0, 1, done + tuple(grads[1, 0]))
-    met[0] = across(outs[0, 1][0])
 
     grad_far, out_back, out_dense, grad_dense = {}, {}, {}, {}
-    for index in (1, 0):
+
+    def unpack_far(index, after):
         count = len(chunks[index])
-        if index == 0:
-            done += tuple(grads[0, 0])
-        grad_far[index] = unpack(spots[index, 1], slots, grads[index, 1], count, after=done)[0]
-        done = (grad_far[index],)
-        grad_far[index] = across(grad_far[index])
-        merged = merge(spots[index, 0], outs[index, 0], met[index], done)
-        done = (merged,)
+        block = unpack(spots[index, 1], slots, grads[index, 1], count, after=after)[0]
+        grad_far[index] = across(block)
+        return (block,)
+
+    def merge_out(index, after):
+        merged = merge(spots[index, 0], outs[index, 0], met[index], after)
         out_back[index] = deal_whole(merged)
-    for index in (1, 0):
+        return (merged,)
+
+    def unpack_near(index, after):
         chunk = chunks[index]
         count = len(chunk)
         out_block = unpack(
-            spots[index, 0], slots, [out_back[index]], count, (), [cot_packed[index]], done
+            spots[index, 0], slots, [out_back[index]], count, (), [cot_packed[index]], after
         )
-        done = (out_block[0],)
         grad_block = unpack(
-            spots[index, 0], slots, grads[index, 0], count, (grad_far[index],), (), done
+            spots[index, 0],
+            slots,
+            grads[index, 0],
+            count,
+            (grad_far[index],),
+            (),
+            (out_block[0],),
         )
-        done = (grad_block[0],)
         for spot, step in enumerate(chunk):
             part_out, part_grad = out_block[spot], grad_block[spot]
             out_dense[step] = along(part_out, -step) if step else part_out
             grad_dense[step] = along(part_grad, -step) if step else part_grad
-        done += tuple(out_dense[step] for step in chunk if step)
+        return (grad_block[0],)
+
+    done = unpack_far(0, done)
+    done = unit(1, 1, done)
+    met[1] = across(outs[1, 1][0])
+    done = merge_out(0, done)
+    done = unpack_far(1, done)
+    done = unpack_near(0, done)
+    done = merge_out(1, done)
+    done = unpack_near(1, done)
 
     expert_total = sum(out_dense[step][:seq_len].astype(jnp.float32) for step in range(line))
     input_total = sum(grad_dense[step].astype(jnp.float32) for step in range(line))

time: 426 us -> 443 us (1.040)
  the two profiles are of different devices: /device:TPU:0 before, /device:TPU:10 now
where the time goes in v2:
time: 443 us; the launch traced here: 434 us
  waiting for transfers between devices  217 us (49%)
  Pallas kernels  89.8 us (20%)
  starting transfers between devices  82.1 us (19%)
  other arithmetic  18.9 us (4%)
  matrix products  14.4 us (3%)
  local copies, waits for them, and re-layouts  10.6 us (2%)
    ppermute x12, waiting for transfers between devices, along(): return lax.ppermute(value, 'expert', pairs)  88.9 us
    ppermute x18, waiting for transfers between devices, deal(): moved.append(lax.ppermute(blocks[d], 'segment', pairs))  52.5 us
    pallas_call x4, Pallas kernels, expert_unit(): pl.pallas_call(partial(expert_kernel, sections, images, split, len(after)...  47.5 us
    ppermute x8, waiting for transfers between devices, across(): return lax.ppermute(value, 'expert', [(j, j ^ 1) for j in range(members)])  44 us
    all_to_all x6, waiting for transfers between devices, deal_whole(): lax.all_to_all(value, 'segment', split_axis=0, concat_axis=0, tiled=True)  31.5 us
    all_to_all x6, starting transfers between devices, deal_whole(): lax.all_to_all(value, 'segment', split_axis=0, concat_axis=0, tiled=True)  31.4 us
    pallas_call x6, Pallas kernels, unpack(): pl.pallas_call(partial(unpack_kernel, images, sections, len(blocks), len(...  19.3 us
    ppermute x12, starting transfers between devices, along(): return lax.ppermute(value, 'expert', pairs)  18.3 us
  transfers between devices with their start and end apart: 46, of which 19 were waited for; matrix products, arithmetic and copies ran while one was open for 6% of the time, Pallas kernels for 17%

profile of v2, /device:TPU:10, one launch (start us, length us, event | category | flops | bytes accessed | tf_op | source)
XLA Modules:
  0.0 434.3 jit_solution(6951448194411469611)
XLA Ops:
  4.1 6.3 %all-to-all-start = ((s32[8,1,704]{2,1,0:T(1,128)}), s32[8,1,704]{2,1,0:T(1,128)S(1)}, u32[]{:S(2)}, u32[]{:S(2)}) async-start(s32[8,1,704]{2,1,0:T(1,128)} %all_to_all.27), calls=%async_computation | async-start | bytes 49152 | tf_op jit(solution)/shard_map/all_to_all | solution.py:397
  15.0 6.6 %convolution_convert_fusion = bf16[128,2496]{0,1:T(8,128)(2,1)} fusion(bf16[1664,2496]{0,1:T(8,128)(2,1)} %param.18, bf16[1,1,128,1664]{3,2,1,0:T(8,128)(2,1)S(1)} %copy-done.3, f32[1664]{0:T(1024)} %param.17, f32[128]{0:T(128)S(1)} %fusion.36, f32[128]{0:T(128)S(1)} %broadcast_multiply_fusion.1), kind=kOutput, calls=%fused_computation.3 | convolution fusion | flops 1064640512 | bytes 9379328 | tf_op jit(solution)/shard_map/jvp()/dot_general | solution.py:34
  23.8 3.8 all-to-all-start.1
  36.3 4.3 all-to-all-start.2
  46.1 12.4 %collective-permute-done.6.refs_3_ = bf16[128,1664]{1,0:T(8,128)(2,1)} collective-permute-done((bf16[128,1664]{1,0:T(8,128)(2,1)}, bf16[128,1664]{1,0:T(8,128)(2,1)}, u32[]{:S(2)}, u32[]{:S(2)}) %collective-permute-start.6) | collective-permute-done | bytes 426016 | tf_op jit(solution)/shard_map/ppermute | solution.py:357
  61.3 4.8 %all-to-all-start.3 = ((bf16[4,96,1664]{2,1,0:T(8,128)(2,1)}), bf16[4,96,1664]{2,1,0:T(8,128)(2,1)}, u32[]{:S(2)}, u32[]{:S(2)}) async-start(bf16[4,96,1664]{2,1,0:T(8,128)(2,1)} %get-tuple-element.65.refs_3_), calls=%async_computation.3 | async-start | bytes 2555904 | tf_op jit(solution)/shard_map/all_to_all | solution.py:370
  75.8 5.6 %all-to-all-done.3.refs_5_.refs_7_ = bf16[4,96,1664]{2,1,0:T(8,128)(2,1)} async-done(((bf16[4,96,1664]{2,1,0:T(8,128)(2,1)}), bf16[4,96,1664]{2,1,0:T(8,128)(2,1)}, u32[]{:S(2)}, u32[]{:S(2)}) %all-to-all-start.3) | async-done | bytes 1277984 | tf_op jit(solution)/shard_map/all_to_all | solution.py:370
  83.4 11.2 %collective-permute-done.2.refs_2_ = bf16[128,1664]{1,0:T(8,128)(2,1)} collective-permute-done((bf16[128,1664]{1,0:T(8,128)(2,1)}, bf16[128,1664]{1,0:T(8,128)(2,1)}, u32[]{:S(2)}, u32[]{:S(2)}) %collective-permute-start.2) | collective-permute-done | bytes 426016 | tf_op jit(solution)/shard_map/ppermute | solution.py:357
  94.6 12.9 %collective-permute-done.3.refs_3_ = bf16[128,1664]{1,0:T(8,128)(2,1)} collective-permute-done((bf16[128,1664]{1,0:T(8,128)(2,1)}, bf16[128,1664]{1,0:T(8,128)(2,1)}, u32[]{:S(2)}, u32[]{:S(2)}) %collective-permute-start.3) | collective-permute-done | bytes 426016 | tf_op jit(solution)/shard_map/ppermute | solution.py:357
  115.7 26.7 %collective-permute-done.10.refs_2_ = bf16[256,1664]{1,0:T(8,128)(2,1)} collective-permute-done((bf16[256,1664]{1,0:T(8,128)(2,1)}, bf16[256,1664]{1,0:T(8,128)(2,1)}, u32[]{:S(2)}, u32[]{:S(2)}) %collective-permute-start.10) | collective-permute-done | bytes 852000 | tf_op jit(solution)/shard_map/ppermute | solution.py:360
  148.0 11.9 %expert.4 = (bf16[96,1664]{1,0:T(8,128)(2,1)}, bf16[96,1664]{1,0:T(8,128)(2,1)}, bf16[96,1664]{1,0:T(8,128)(2,1)}, bf16[96,1664]{1,0:T(8,128)(2,1)}, bf16[4,96,1664]{2,1,0:T(8,128)(2,1)}) custom-call(s32[7]{0:T(128)} %get-tuple-element.130.refs_0_.spots_ref, s32[4,8,48]{2,1,0:T(8,128)} %reshape.209.refs_1_, bf16[1664,8]{1,0:T(8,128)(2,1)} %copy.60.refs_2_, ...), custom_call_target="tpu_custom_call" | custom-call | flops 1000 | bytes 1000 | tf_op jit(solution)/shard_map/expert/pallas_call | solution.py:296
  161.8 11.8 %expert.5 = (bf16[384,1664]{1,0:T(8,128)(2,1)}, bf16[96,1664]{1,0:T(8,128)(2,1)}, bf16[96,1664]{1,0:T(8,128)(2,1)}, bf16[96,1664]{1,0:T(8,128)(2,1)}, bf16[96,1664]{1,0:T(8,128)(2,1)}) custom-call(s32[7]{0:T(128)} %get-tuple-element.129.refs_0_, s32[4,8,48]{2,1,0:T(8,128)} %reshape.209.refs_1_, bf16[1664,8]{1,0:T(8,128)(2,1)} %copy.60.refs_2_, ...), custom_call_target="tpu_custom_call" | custom-call | flops 1000 | bytes 1000 | tf_op jit(solution)/shard_map/expert/pallas_call | solution.py:296
  178.5 7.8 %collective-permute-done.8.refs_5_ = bf16[96,1664]{1,0:T(8,128)(2,1)} collective-permute-done((bf16[96,1664]{1,0:T(8,128)(2,1)}, bf16[96,1664]{1,0:T(8,128)(2,1)}, u32[]{:S(2)}, u32[]{:S(2)}) %collective-permute-start.8) | collective-permute-done | bytes 319520 | tf_op jit(solution)/shard_map/ppermute | solution.py:366
  186.7 5.7 %collective-permute-done.9.refs_6_ = bf16[96,1664]{1,0:T(8,128)(2,1)} collective-permute-done((bf16[96,1664]{1,0:T(8,128)(2,1)}, bf16[96,1664]{1,0:T(8,128)(2,1)}, u32[]{:S(2)}, u32[]{:S(2)}) %collective-permute-start.9) | collective-permute-done | bytes 319520 | tf_op jit(solution)/shard_map/ppermute | solution.py:366
  193.2 11.9 %expert.6 = (bf16[96,1664]{1,0:T(8,128)(2,1)}, bf16[96,1664]{1,0:T(8,128)(2,1)}, bf16[96,1664]{1,0:T(8,128)(2,1)}, bf16[96,1664]{1,0:T(8,128)(2,1)}, bf16[4,96,1664]{2,1,0:T(8,128)(2,1)}) custom-call(s32[7]{0:T(128)} %add_add_fusion.4.refs_0_.spots_ref, s32[4,8,48]{2,1,0:T(8,128)} %reshape.209.refs_1_, bf16[1664,8]{1,0:T(8,128)(2,1)} %copy.60.refs_2_, ...), custom_call_target="tpu_custom_call" | custom-call | flops 1000 | bytes 1000 | tf_op jit(solution)/shard_map/expert/pallas_call | solution.py:296
  205.2 17.3 %collective-permute-done.18.refs_2_ = bf16[256,1664]{1,0:T(8,128)(2,1)} collective-permute-done((bf16[256,1664]{1,0:T(8,128)(2,1)}, bf16[256,1664]{1,0:T(8,128)(2,1)}, u32[]{:S(2)}, u32[]{:S(2)}) %collective-permute-start.18) | collective-permute-done | bytes 852000 | tf_op jit(solution)/shard_map/ppermute | solution.py:360
  230.0 5.9 %collective-permute-done.20.refs_5_ = bf16[96,1664]{1,0:T(8,128)(2,1)} collective-permute-done((bf16[96,1664]{1,0:T(8,128)(2,1)}, bf16[96,1664]{1,0:T(8,128)(2,1)}, u32[]{:S(2)}, u32[]{:S(2)}) %collective-permute-start.20) | collective-permute-done | bytes 319520 | tf_op jit(solution)/shard_map/ppermute | solution.py:366
  235.9 5.9 %collective-permute-done.21.refs_6_ = bf16[96,1664]{1,0:T(8,128)(2,1)} collective-permute-done((bf16[96,1664]{1,0:T(8,128)(2,1)}, bf16[96,1664]{1,0:T(8,128)(2,1)}, u32[]{:S(2)}, u32[]{:S(2)}) %collective-permute-start.21) | collective-permute-done | bytes 319520 | tf_op jit(solution)/shard_map/ppermute | solution.py:366
  241.8 11.8 %expert.7 = (bf16[384,1664]{1,0:T(8,128)(2,1)}, bf16[96,1664]{1,0:T(8,128)(2,1)}, bf16[96,1664]{1,0:T(8,128)(2,1)}, bf16[96,1664]{1,0:T(8,128)(2,1)}, bf16[96,1664]{1,0:T(8,128)(2,1)}) custom-call(s32[7]{0:T(128)} %get-tuple-element.128.refs_0_, s32[4,8,48]{2,1,0:T(8,128)} %reshape.209.refs_1_, bf16[1664,8]{1,0:T(8,128)(2,1)} %copy.60.refs_2_, ...), custom_call_target="tpu_custom_call" | custom-call | flops 1000 | bytes 1000 | tf_op jit(solution)/shard_map/expert/pallas_call | solution.py:296
  256.7 4.6 %all-to-all-start.5 = ((bf16[4,96,1664]{2,1,0:T(8,128)(2,1)}), bf16[4,96,1664]{2,1,0:T(8,128)(2,1)}, u32[]{:S(2)}, u32[]{:S(2)}) async-start(bf16[4,96,1664]{2,1,0:T(8,128)(2,1)} %merge.2.refs_6_), calls=%async_computation.5 | async-start | bytes 2555904 | tf_op jit(solution)/shard_map/all_to_all | solution.py:370
  263.0 13.6 %all-to-all-done.5.refs_2_ = bf16[4,96,1664]{2,1,0:T(8,128)(2,1)} async-done(((bf16[4,96,1664]{2,1,0:T(8,128)(2,1)}), bf16[4,96,1664]{2,1,0:T(8,128)(2,1)}, u32[]{:S(2)}, u32[]{:S(2)}) %all-to-all-start.5) | async-done | bytes 1277984 | tf_op jit(solution)/shard_map/all_to_all | solution.py:370
  276.6 6.0 %all-to-all-start.4 = ((bf16[4,96,1664]{2,1,0:T(8,128)(2,1)}), bf16[4,96,1664]{2,1,0:T(8,128)(2,1)}, u32[]{:S(2)}, u32[]{:S(2)}) async-start(bf16[4,96,1664]{2,1,0:T(8,128)(2,1)} %get-tuple-element.81.refs_10_), calls=%async_computation.4 | async-start | bytes 2555904 | tf_op jit(solution)/shard_map/all_to_all | solution.py:370
  286.2 18.8 %collective-permute-done.29.refs_4_ = bf16[96,1664]{1,0:T(8,128)(2,1)} collective-permute-done((bf16[96,1664]{1,0:T(8,128)(2,1)}, bf16[96,1664]{1,0:T(8,128)(2,1)}, u32[]{:S(2)}, u32[]{:S(2)}) %collective-permute-start.29) | collective-permute-done | bytes 319520 | tf_op jit(solution)/shard_map/ppermute | solution.py:366
  305.0 6.4 %collective-permute-done.30.refs_5_ = bf16[96,1664]{1,0:T(8,128)(2,1)} collective-permute-done((bf16[96,1664]{1,0:T(8,128)(2,1)}, bf16[96,1664]{1,0:T(8,128)(2,1)}, u32[]{:S(2)}, u32[]{:S(2)}) %collective-permute-start.30) | collective-permute-done | bytes 319520 | tf_op jit(solution)/shard_map/ppermute | solution.py:366
  314.3 3.6 unpack.8
  324.2 5.8 %all-to-all-start.6 = ((bf16[4,96,1664]{2,1,0:T(8,128)(2,1)}), bf16[4,96,1664]{2,1,0:T(8,128)(2,1)}, u32[]{:S(2)}, u32[]{:S(2)}) async-start(bf16[4,96,1664]{2,1,0:T(8,128)(2,1)} %merge.3.refs_4_), calls=%async_computation.6 | async-start | bytes 2555904 | tf_op jit(solution)/shard_map/all_to_all | solution.py:370
  333.1 12.3 %all-to-all-done.6.refs_2_ = bf16[4,96,1664]{2,1,0:T(8,128)(2,1)} async-done(((bf16[4,96,1664]{2,1,0:T(8,128)(2,1)}), bf16[4,96,1664]{2,1,0:T(8,128)(2,1)}, u32[]{:S(2)}, u32[]{:S(2)}) %all-to-all-start.6) | async-done | bytes 1277984 | tf_op jit(solution)/shard_map/all_to_all | solution.py:370
  345.3 5.9 %all-to-all-start.7 = ((bf16[4,96,1664]{2,1,0:T(8,128)(2,1)}), bf16[4,96,1664]{2,1,0:T(8,128)(2,1)}, u32[]{:S(2)}, u32[]{:S(2)}) async-start(bf16[4,96,1664]{2,1,0:T(8,128)(2,1)} %get-tuple-element.88.refs_3_), calls=%async_computation.7 | async-start | bytes 2555904 | tf_op jit(solution)/shard_map/all_to_all | solution.py:370
  355.6 3.5 unpack.10
  360.9 32.5 %collective-permute-done.32 = bf16[144,1664]{1,0:T(8,128)(2,1)S(1)} collective-permute-done((bf16[144,1664]{1,0:T(8,128)(2,1)}, bf16[144,1664]{1,0:T(8,128)(2,1)S(1)}, u32[]{:S(2)}, u32[]{:S(2)}) %collective-permute-start.32) | collective-permute-done | bytes 479264 | tf_op jit(solution)/shard_map/ppermute | solution.py:357
  401.1 13.2 %collective-permute-done.31 = bf16[144,1664]{1,0:T(8,128)(2,1)} collective-permute-done((bf16[144,1664]{1,0:T(8,128)(2,1)}, bf16[144,1664]{1,0:T(8,128)(2,1)}, u32[]{:S(2)}, u32[]{:S(2)}) %collective-permute-start.31) | collective-permute-done | bytes 479264 | tf_op jit(solution)/shard_map/ppermute | solution.py:357
  416.3 4.5 %collective-permute-done.36 = bf16[128,1664]{1,0:T(8,128)(2,1)} collective-permute-done((bf16[128,1664]{1,0:T(8,128)(2,1)}, bf16[128,1664]{1,0:T(8,128)(2,1)}, u32[]{:S(2)}, u32[]{:S(2)}) %collective-permute-start.36) | collective-permute-done | bytes 426016 | tf_op jit(solution)/shard_map/ppermute | solution.py:357
  (205 shorter events, 117.5 us)
Async XLA Ops:
  10.3 23.2 %collective-permute-start = (bf16[128,1664]{1,0:T(8,128)(2,1)}, bf16[128,1664]{1,0:T(8,128)(2,1)}, u32[]{:S(2)}, u32[]{:S(2)}) collective-permute-start(bf16[128,1664]{1,0:T(8,128)(2,1)} %bitcast.99), channel_id=1, source_target_pairs={{0,8},{4,12},{8,16},{12,20},{16,24},{20,28},{24,0},{28,4},{1,9},{5... | collective-permute-start | bytes 1277960 | tf_op jit(solution)/shard_map/ppermute | solution.py:357
  30.5 28.0 %collective-permute-start.6 = (bf16[128,1664]{1,0:T(8,128)(2,1)}, bf16[128,1664]{1,0:T(8,128)(2,1)}, u32[]{:S(2)}, u32[]{:S(2)}) collective-permute-start(bf16[128,1664]{1,0:T(8,128)(2,1)} %bitcast.101), channel_id=1, source_target_pairs={{0,16},{4,20},{8,24},{12,28},{16,0},{20,4},{24,8},{28,12},{1,17},{... | collective-permute-start | bytes 1277960 | tf_op jit(solution)/shard_map/ppermute | solution.py:357
  36.3 24.9 %all-to-all-start.2 = ((bf16[4,96,1664]{2,1,0:T(8,128)(2,1)}), bf16[4,96,1664]{2,1,0:T(8,128)(2,1)}, u32[]{:S(2)}, u32[]{:S(2)}) async-start(bf16[4,96,1664]{2,1,0:T(8,128)(2,1)} %get-tuple-element.63.refs_3_), calls=%async_computation.2 | async-start | bytes 2555904 | tf_op jit(solution)/shard_map/all_to_all | solution.py:370
  61.3 20.2 %all-to-all-start.3 = ((bf16[4,96,1664]{2,1,0:T(8,128)(2,1)}), bf16[4,96,1664]{2,1,0:T(8,128)(2,1)}, u32[]{:S(2)}, u32[]{:S(2)}) async-start(bf16[4,96,1664]{2,1,0:T(8,128)(2,1)} %get-tuple-element.65.refs_3_), calls=%async_computation.3 | async-start | bytes 2555904 | tf_op jit(solution)/shard_map/all_to_all | solution.py:370
  66.1 41.4 %collective-permute-start.4 = (bf16[4,96,1664]{2,1,0:T(8,128)(2,1)}, bf16[4,96,1664]{2,1,0:T(8,128)(2,1)}, u32[]{:S(2)}, u32[]{:S(2)}) collective-permute-start(bf16[4,96,1664]{2,1,0:T(8,128)(2,1)} %all-to-all-done.2.refs_7_), channel_id=1, source_target_pairs={{0,4},{4,0},{8,12},{12,8},{16,20},{20,16},{24,28},{28,24},{1,5},{5... | collective-permute-start | bytes 3833864 | tf_op jit(solution)/shard_map/ppermute | solution.py:360
  70.4 24.2 %collective-permute-start.2 = (bf16[128,1664]{1,0:T(8,128)(2,1)}, bf16[128,1664]{1,0:T(8,128)(2,1)}, u32[]{:S(2)}, u32[]{:S(2)}) collective-permute-start(bf16[128,1664]{1,0:T(8,128)(2,1)} %multiply_convert_fusion.refs_3_), channel_id=1, source_target_pairs={{0,24},{4,28},{8,0},{12,4},{16,8},{20,12},{24,16},{28,20},{1,25},{... | collective-permute-start | bytes 1277960 | tf_op jit(solution)/shard_map/ppermute | solution.py:357
  72.4 35.1 %collective-permute-start.3 = (bf16[128,1664]{1,0:T(8,128)(2,1)}, bf16[128,1664]{1,0:T(8,128)(2,1)}, u32[]{:S(2)}, u32[]{:S(2)}) collective-permute-start(bf16[128,1664]{1,0:T(8,128)(2,1)} %multiply_convert_fusion.refs_3_), channel_id=1, source_target_pairs={{0,16},{4,20},{8,24},{12,28},{16,0},{20,4},{24,8},{28,12},{1,17},{... | collective-permute-start | bytes 1277960 | tf_op jit(solution)/shard_map/ppermute | solution.py:357
  81.4 63.7 %collective-permute-start.14 = (bf16[4,96,1664]{2,1,0:T(8,128)(2,1)}, bf16[4,96,1664]{2,1,0:T(8,128)(2,1)}, u32[]{:S(2)}, u32[]{:S(2)}) collective-permute-start(bf16[4,96,1664]{2,1,0:T(8,128)(2,1)} %all-to-all-done.3.refs_5_.refs_7_), channel_id=1, source_target_pairs={{0,4},{4,0},{8,12},{12,8},{16,20},{20,16},{24,28},{28,24},{1,5},{5... | collective-permute-start | bytes 3833864 | tf_op jit(solution)/shard_map/ppermute | solution.py:360
  110.5 31.9 %collective-permute-start.10 = (bf16[256,1664]{1,0:T(8,128)(2,1)}, bf16[256,1664]{1,0:T(8,128)(2,1)}, u32[]{:S(2)}, u32[]{:S(2)}) collective-permute-start(bf16[256,1664]{1,0:T(8,128)(2,1)} %get-tuple-element.71), channel_id=1, source_target_pairs={{0,4},{4,0},{8,12},{12,8},{16,20},{20,16},{24,28},{28,24},{1,5},{5... | collective-permute-start | bytes 2555912 | tf_op jit(solution)/shard_map/ppermute | solution.py:360
  110.9 34.7 %collective-permute-start.15 = (bf16[96,1664]{1,0:T(8,128)(2,1)}, bf16[96,1664]{1,0:T(8,128)(2,1)}, u32[]{:S(2)}, u32[]{:S(2)}) collective-permute-start(bf16[96,1664]{1,0:T(8,128)(2,1)} %get-tuple-element.78), channel_id=1, source_target_pairs={{0,1},{1,0},{2,3},{3,2},{4,5},{5,4},{6,7},{7,6},{8,9},{9,8},{10,11... | collective-permute-start | bytes 958472 | tf_op jit(solution)/shard_map/ppermute | solution.py:366
  110.9 37.1 %collective-permute-start.16 = (bf16[96,1664]{1,0:T(8,128)(2,1)}, bf16[96,1664]{1,0:T(8,128)(2,1)}, u32[]{:S(2)}, u32[]{:S(2)}) collective-permute-start(bf16[96,1664]{1,0:T(8,128)(2,1)} %get-tuple-element.79), channel_id=1, source_target_pairs={{0,2},{1,3},{2,0},{3,1},{4,6},{5,7},{6,4},{7,5},{8,10},{9,11},{10,... | collective-permute-start | bytes 958472 | tf_op jit(solution)/shard_map/ppermute | solution.py:366
  111.3 36.7 %collective-permute-start.17 = (bf16[96,1664]{1,0:T(8,128)(2,1)}, bf16[96,1664]{1,0:T(8,128)(2,1)}, u32[]{:S(2)}, u32[]{:S(2)}) collective-permute-start(bf16[96,1664]{1,0:T(8,128)(2,1)} %get-tuple-element.80), channel_id=1, source_target_pairs={{0,3},{1,2},{2,1},{3,0},{4,7},{5,6},{6,5},{7,4},{8,11},{9,10},{10,... | collective-permute-start | bytes 958472 | tf_op jit(solution)/shard_map/ppermute | solution.py:366
  173.6 80.0 %collective-permute-start.27 = (bf16[384,1664]{1,0:T(8,128)(2,1)}, bf16[384,1664]{1,0:T(8,128)(2,1)}, u32[]{:S(2)}, u32[]{:S(2)}) collective-permute-start(bf16[384,1664]{1,0:T(8,128)(2,1)} %get-tuple-element.101), channel_id=1, source_target_pairs={{0,4},{4,0},{8,12},{12,8},{16,20},{20,16},{24,28},{28,24},{1,5},{5... | collective-permute-start | bytes 3833864 | tf_op jit(solution)/shard_map/ppermute | solution.py:360
  175.4 47.1 %collective-permute-start.18 = (bf16[256,1664]{1,0:T(8,128)(2,1)}, bf16[256,1664]{1,0:T(8,128)(2,1)}, u32[]{:S(2)}, u32[]{:S(2)}) collective-permute-start(bf16[256,1664]{1,0:T(8,128)(2,1)} %get-tuple-element.87), channel_id=1, source_target_pairs={{0,4},{4,0},{8,12},{12,8},{16,20},{20,16},{24,28},{28,24},{1,5},{5... | collective-permute-start | bytes 2555912 | tf_op jit(solution)/shard_map/ppermute | solution.py:360
  178.2 46.9 %collective-permute-start.22 = (bf16[96,1664]{1,0:T(8,128)(2,1)}, bf16[96,1664]{1,0:T(8,128)(2,1)S(1)}, u32[]{:S(2)}, u32[]{:S(2)}) collective-permute-start(bf16[96,1664]{1,0:T(8,128)(2,1)} %get-tuple-element.93), channel_id=1, source_target_pairs={{0,1},{1,0},{2,3},{3,2},{4,5},{5,4},{6,7},{7,6},{8,9},{9,8},{10,11... | collective-permute-start | bytes 958472 | tf_op jit(solution)/shard_map/ppermute | solution.py:366
  186.3 39.3 %collective-permute-start.23 = (bf16[96,1664]{1,0:T(8,128)(2,1)}, bf16[96,1664]{1,0:T(8,128)(2,1)}, u32[]{:S(2)}, u32[]{:S(2)}) collective-permute-start(bf16[96,1664]{1,0:T(8,128)(2,1)} %get-tuple-element.94), channel_id=1, source_target_pairs={{0,2},{1,3},{2,0},{3,1},{4,6},{5,7},{6,4},{7,5},{8,10},{9,11},{10,... | collective-permute-start | bytes 958472 | tf_op jit(solution)/shard_map/ppermute | solution.py:366
  192.4 34.7 %collective-permute-start.24 = (bf16[96,1664]{1,0:T(8,128)(2,1)}, bf16[96,1664]{1,0:T(8,128)(2,1)}, u32[]{:S(2)}, u32[]{:S(2)}) collective-permute-start(bf16[96,1664]{1,0:T(8,128)(2,1)} %get-tuple-element.95), channel_id=1, source_target_pairs={{0,3},{1,2},{2,1},{3,0},{4,7},{5,6},{6,5},{7,4},{8,11},{9,10},{10,... | collective-permute-start | bytes 958472 | tf_op jit(solution)/shard_map/ppermute | solution.py:366
  256.7 20.0 %all-to-all-start.5 = ((bf16[4,96,1664]{2,1,0:T(8,128)(2,1)}), bf16[4,96,1664]{2,1,0:T(8,128)(2,1)}, u32[]{:S(2)}, u32[]{:S(2)}) async-start(bf16[4,96,1664]{2,1,0:T(8,128)(2,1)} %merge.2.refs_6_), calls=%async_computation.5 | async-start | bytes 2555904 | tf_op jit(solution)/shard_map/all_to_all | solution.py:370
  261.3 59.8 %collective-permute-start.25 = (bf16[384,1664]{1,0:T(8,128)(2,1)}, bf16[384,1664]{1,0:T(8,128)(2,1)}, u32[]{:S(2)}, u32[]{:S(2)}) collective-permute-start(bf16[384,1664]{1,0:T(8,128)(2,1)} %get-tuple-element.96), channel_id=1, source_target_pairs={{0,4},{4,0},{8,12},{12,8},{16,20},{20,16},{24,28},{28,24},{1,5},{5... | collective-permute-start | bytes 3833864 | tf_op jit(solution)/shard_map/ppermute | solution.py:360
  276.6 41.2 %all-to-all-start.4 = ((bf16[4,96,1664]{2,1,0:T(8,128)(2,1)}), bf16[4,96,1664]{2,1,0:T(8,128)(2,1)}, u32[]{:S(2)}, u32[]{:S(2)}) async-start(bf16[4,96,1664]{2,1,0:T(8,128)(2,1)} %get-tuple-element.81.refs_10_), calls=%async_computation.4 | async-start | bytes 2555904 | tf_op jit(solution)/shard_map/all_to_all | solution.py:370
  282.6 35.3 %collective-permute-start.26 = (bf16[256,1664]{1,0:T(8,128)(2,1)}, bf16[256,1664]{1,0:T(8,128)(2,1)}, u32[]{:S(2)}, u32[]{:S(2)}) collective-permute-start(bf16[256,1664]{1,0:T(8,128)(2,1)} %unpack.6.refs_10_), channel_id=1, source_target_pairs={{0,4},{4,0},{8,12},{12,8},{16,20},{20,16},{24,28},{28,24},{1,5},{5... | collective-permute-start | bytes 2555912 | tf_op jit(solution)/shard_map/ppermute | solution.py:360
  284.3 20.7 %collective-permute-start.29 = (bf16[96,1664]{1,0:T(8,128)(2,1)}, bf16[96,1664]{1,0:T(8,128)(2,1)}, u32[]{:S(2)}, u32[]{:S(2)}) collective-permute-start(bf16[96,1664]{1,0:T(8,128)(2,1)} %get-tuple-element.104), channel_id=1, source_target_pairs={{0,2},{1,3},{2,0},{3,1},{4,6},{5,7},{6,4},{7,5},{8,10},{9,11},{10,... | collective-permute-start | bytes 958472 | tf_op jit(solution)/shard_map/ppermute | solution.py:366
  284.6 26.9 %collective-permute-start.30 = (bf16[96,1664]{1,0:T(8,128)(2,1)}, bf16[96,1664]{1,0:T(8,128)(2,1)}, u32[]{:S(2)}, u32[]{:S(2)}) collective-permute-start(bf16[96,1664]{1,0:T(8,128)(2,1)} %get-tuple-element.105), channel_id=1, source_target_pairs={{0,3},{1,2},{2,1},{3,0},{4,7},{5,6},{6,5},{7,4},{8,11},{9,10},{10,... | collective-permute-start | bytes 958472 | tf_op jit(solution)/shard_map/ppermute | solution.py:366
  324.2 21.2 %all-to-all-start.6 = ((bf16[4,96,1664]{2,1,0:T(8,128)(2,1)}), bf16[4,96,1664]{2,1,0:T(8,128)(2,1)}, u32[]{:S(2)}, u32[]{:S(2)}) async-start(bf16[4,96,1664]{2,1,0:T(8,128)(2,1)} %merge.3.refs_4_), calls=%async_computation.6 | async-start | bytes 2555904 | tf_op jit(solution)/shard_map/all_to_all | solution.py:370
  331.3 63.0 %collective-permute-start.34 = (bf16[256,1664]{1,0:T(8,128)(2,1)}, bf16[256,1664]{1,0:T(8,128)(2,1)}, u32[]{:S(2)}, u32[]{:S(2)}) collective-permute-start(bf16[256,1664]{1,0:T(8,128)(2,1)} %unpack.7.refs_4_), channel_id=1, source_target_pairs={{0,4},{4,0},{8,12},{12,8},{16,20},{20,16},{24,28},{28,24},{1,5},{5... | collective-permute-start | bytes 2555912 | tf_op jit(solution)/shard_map/ppermute | solution.py:360
  333.1 26.1 %collective-permute-start.33 = (bf16[144,1664]{1,0:T(8,128)(2,1)}, bf16[144,1664]{1,0:T(8,128)(2,1)}, u32[]{:S(2)}, u32[]{:S(2)}) collective-permute-start(bf16[144,1664]{1,0:T(8,128)(2,1)} %get-tuple-element.106.refs_4_), channel_id=1, source_target_pairs={{0,8},{4,12},{8,16},{12,20},{16,24},{20,28},{24,0},{28,4},{1,9},{5... | collective-permute-start | bytes 1437704 | tf_op jit(solution)/shard_map/ppermute | solution.py:357
  345.3 48.9 %all-to-all-start.7 = ((bf16[4,96,1664]{2,1,0:T(8,128)(2,1)}), bf16[4,96,1664]{2,1,0:T(8,128)(2,1)}, u32[]{:S(2)}, u32[]{:S(2)}) async-start(bf16[4,96,1664]{2,1,0:T(8,128)(2,1)} %get-tuple-element.88.refs_3_), calls=%async_computation.7 | async-start | bytes 2555904 | tf_op jit(solution)/shard_map/all_to_all | solution.py:370
  351.3 42.2 %collective-permute-start.32 = (bf16[144,1664]{1,0:T(8,128)(2,1)}, bf16[144,1664]{1,0:T(8,128)(2,1)S(1)}, u32[]{:S(2)}, u32[]{:S(2)}) collective-permute-start(bf16[144,1664]{1,0:T(8,128)(2,1)} %get-tuple-element.110), channel_id=1, source_target_pairs={{0,16},{4,20},{8,24},{12,28},{16,0},{20,4},{24,8},{28,12},{1,17},{... | collective-permute-start | bytes 1437704 | tf_op jit(solution)/shard_map/ppermute | solution.py:357
  354.7 66.1 %collective-permute-start.37 = (bf16[128,1664]{1,0:T(8,128)(2,1)}, bf16[128,1664]{1,0:T(8,128)(2,1)}, u32[]{:S(2)}, u32[]{:S(2)}) collective-permute-start(bf16[128,1664]{1,0:T(8,128)(2,1)} %get-tuple-element.107.refs_5_), channel_id=1, source_target_pairs={{0,8},{4,12},{8,16},{12,20},{16,24},{20,28},{24,0},{28,4},{1,9},{5... | collective-permute-start | bytes 1277960 | tf_op jit(solution)/shard_map/ppermute | solution.py:357
  354.7 66.0 %collective-permute-start.36 = (bf16[128,1664]{1,0:T(8,128)(2,1)}, bf16[128,1664]{1,0:T(8,128)(2,1)}, u32[]{:S(2)}, u32[]{:S(2)}) collective-permute-start(bf16[128,1664]{1,0:T(8,128)(2,1)} %get-tuple-element.113), channel_id=1, source_target_pairs={{0,16},{4,20},{8,24},{12,28},{16,0},{20,4},{24,8},{28,12},{1,17},{... | collective-permute-start | bytes 1277960 | tf_op jit(solution)/shard_map/ppermute | solution.py:357
  359.1 55.2 %collective-permute-start.31 = (bf16[144,1664]{1,0:T(8,128)(2,1)}, bf16[144,1664]{1,0:T(8,128)(2,1)}, u32[]{:S(2)}, u32[]{:S(2)}) collective-permute-start(bf16[144,1664]{1,0:T(8,128)(2,1)} %get-tuple-element.109.refs_4_), channel_id=1, source_target_pairs={{0,24},{4,28},{8,0},{12,4},{16,8},{20,12},{24,16},{28,20},{1,25},{... | collective-permute-start | bytes 1437704 | tf_op jit(solution)/shard_map/ppermute | solution.py:357
  397.4 25.6 %collective-permute-start.35 = (bf16[128,1664]{1,0:T(8,128)(2,1)}, bf16[128,1664]{1,0:T(8,128)(2,1)}, u32[]{:S(2)}, u32[]{:S(2)}) collective-permute-start(bf16[128,1664]{1,0:T(8,128)(2,1)} %get-tuple-element.112), channel_id=1, source_target_pairs={{0,24},{4,28},{8,0},{12,4},{16,8},{20,12},{24,16},{28,20},{1,25},{... | collective-permute-start | bytes 1277960 | tf_op jit(solution)/shard_map/ppermute | solution.py:357
  (38 other events, 351.3 us)
